TPU v7x, 512 devices: a whole 4x8x8 slice. The times are simulated.
512 devices in a mesh: ctx: 64 (over y, x, core), head: 8 (over z).
Axes of the slice: x: 4, y: 8, z: 8, core: 2. Of those that a mesh axis runs over, the one named last changes fastest.
Arguments:
- queries: bfloat16 [8192, 8192], P('ctx', 'head'), may hold values from -21 to 21
- key_cache: bfloat16 [32768, 1024], P('ctx', 'head'), may hold values from -21 to 21
- value_cache: bfloat16 [32768, 1024], P('ctx', 'head'), may hold values from -18 to 18
- offsets: int32 [1024], P('ctx'), may hold values from 0 to 504
- selected: int32 [1024, 8], P('ctx'), may hold values from -1 to 63, as said below
- out_gain: bfloat16 [8192], P('head'), may hold values from 0.5 to 1.5
Outputs:
- normed_out: bfloat16 [8192, 8192], P('ctx', 'head')
Inputs may be any that keep to these rules, and one draw needn't show every extreme that they name: Entry 0 of row g is the query block's own key block g // 16; the other entries are distinct key blocks below it, followed by -1 for unused entries. Among the query blocks of one index of ctx, at most 2 select any one key block in entries 1 and later, and some device has a block selected exactly 2 times by one device's query blocks.
All inputs are finite; a program needn't handle non-finite values.
Results may differ from a plain program's by a relative error of at most 0.01.
Values may be sent and summed in bfloat16 or wider, within the bound.
No kernel may reach another device: no remote copies, remote signals or barrier semaphores. Data moves between devices by JAX's collectives and lax.ppermute only.
A program may use at most 64 MiB of HBM per device.

v0:
```python
import math

import jax
import jax.numpy as jnp
from jax import lax
from jax.sharding import PartitionSpec as P

HD = 128
GROUP = 8
CAP = 2
FEAT = 8192


def attend(query_rows, key_block, value_block, visible):
    scaling = 1.0 / math.sqrt(HD)
    scores = (
        jnp.einsum("nkgd,jkd->nkgj", query_rows, key_block, preferred_element_type=jnp.float32)
        * scaling
    )
    if visible is not None:
        scores = jnp.where(visible, scores, -jnp.inf)
    row_peak = jnp.max(scores, axis=-1)
    weights = jnp.exp(scores - row_peak[..., None])
    row_total = jnp.sum(weights, axis=-1)
    probability = weights.astype(jnp.bfloat16)
    mixed_out = jnp.einsum(
        "nkgj,jkd->nkgd", probability, value_block, preferred_element_type=jnp.float32
    )
    mixed_out = mixed_out / row_total[..., None]
    return (mixed_out.astype(jnp.bfloat16), row_peak, row_total)


def send_back(mixed_out, row_peak, row_total):
    return (
        lax.all_to_all(
            mixed_out.astype(jnp.float32), "ctx", split_axis=0, concat_axis=0, tiled=True
        ).astype(mixed_out.dtype),
        lax.all_to_all(row_peak, "ctx", split_axis=0, concat_axis=0, tiled=True),
        lax.all_to_all(row_total, "ctx", split_axis=0, concat_axis=0, tiled=True),
    )


def serve_all(received, key_block, value_block):
    sources, count, block_rows, features = received.shape
    heads_local = key_block.shape[1]
    total_rows = sources * count * block_rows
    step_rows = math.gcd(total_rows, 256)
    grouped = received.reshape(total_rows // step_rows, step_rows, heads_local, GROUP, HD)

    def run_rows(row_block):
        return attend(row_block, key_block, value_block, None)

    mixed_out, row_peak, row_total = lax.map(run_rows, grouped)
    head_count = heads_local * GROUP
    return (
        mixed_out.reshape(sources, count, block_rows, features),
        row_peak.reshape(sources, count, block_rows, head_count),
        row_total.reshape(sources, count, block_rows, head_count),
    )


def body(queries, key_cache, value_cache, offsets, selected, out_gain):
    row_count, features = queries.shape
    blocks_local = offsets.shape[0]
    block_rows = row_count // blocks_local
    block_len = key_cache.shape[0]
    heads_local = key_cache.shape[1] // HD
    head_count = heads_local * GROUP
    devices = lax.axis_size("ctx")
    key_block = key_cache.reshape(block_len, heads_local, HD)
    value_block = value_cache.reshape(block_len, heads_local, HD)
    query_rows = queries.reshape(row_count, heads_local, GROUP, HD)
    last_key = (offsets[:, None] + jnp.arange(block_rows, dtype=jnp.int32)[None, :]).reshape(
        row_count
    )
    causal = (jnp.arange(block_len, dtype=jnp.int32)[None, :] <= last_key[:, None])[
        :, None, None, :
    ]
    own_mixed, own_peak, own_total = attend(query_rows, key_block, value_block, causal)
    own_peak = own_peak.reshape(blocks_local, block_rows, head_count)
    own_total = own_total.reshape(blocks_local, block_rows, head_count)
    own_mixed = own_mixed.reshape(blocks_local, block_rows, head_count, HD).astype(jnp.float32)
    remote = selected[:, 1:]
    query_flat = queries.reshape(blocks_local, block_rows * features)
    targets = jnp.arange(devices, dtype=jnp.int32)
    hit_count = jnp.sum((remote[:, :, None] == targets[None, None, :]).astype(jnp.int32), axis=1)
    slot_of = jnp.cumsum(hit_count, axis=0) - hit_count
    placed = (hit_count[:, :, None] == 1) & (
        slot_of[:, :, None] == jnp.arange(CAP, dtype=jnp.int32)[None, None, :]
    )
    outgoing = jnp.einsum(
        "gdc,gf->dcf", placed.astype(jnp.bfloat16), query_flat, preferred_element_type=jnp.float32
    ).astype(jnp.bfloat16)
    outgoing = outgoing.reshape(devices, CAP, block_rows, features)
    mixed_out, row_peak, row_total = serve_all(
        lax.all_to_all(outgoing, "ctx", split_axis=0, concat_axis=0, tiled=True),
        key_block,
        value_block,
    )
    back_mixed, back_peak, back_total = send_back(mixed_out, row_peak, row_total)
    safe_block = jnp.maximum(remote, 0)
    slot_at = jnp.take_along_axis(slot_of, safe_block, axis=1)
    flat_index = safe_block * CAP + slot_at
    is_valid = (remote >= 0)[:, :, None, None]
    got_mixed = back_mixed.reshape(devices * CAP, block_rows, head_count, HD)[flat_index]
    got_peak = back_peak.reshape(devices * CAP, block_rows, head_count)[flat_index]
    got_total = back_total.reshape(devices * CAP, block_rows, head_count)[flat_index]
    masked_peak = jnp.where(is_valid, got_peak, -jnp.inf)
    peak_all = jnp.maximum(own_peak, jnp.max(masked_peak, axis=1))
    weight = jnp.where(is_valid, got_total * jnp.exp(masked_peak - peak_all[:, None]), 0.0)
    own_weight = own_total * jnp.exp(own_peak - peak_all)
    numerator = own_weight[..., None] * own_mixed + jnp.sum(
        weight[..., None] * got_mixed.astype(jnp.float32), axis=1
    )
    denominator = own_weight + jnp.sum(weight, axis=1)
    attended = (numerator / denominator[..., None]).reshape(row_count, features)
    squares = lax.psum(jnp.sum(attended * attended, axis=-1), "head")
    scaling = lax.rsqrt(squares / FEAT + 1e-06)
    normed = attended * scaling[:, None] * out_gain.astype(jnp.float32)[None, :]
    return normed.astype(jnp.bfloat16)


def solution(mesh):
    placed = (
        P("ctx", "head"),
        P("ctx", "head"),
        P("ctx", "head"),
        P("ctx"),
        P("ctx", None),
        P("head"),
    )
    return jax.shard_map(
        body, mesh=mesh, in_specs=placed, out_specs=P("ctx", "head"), check_vma=False
    )
```

profile of v0, /device:TPU:56, one launch (start us, length us, event | category | flops | bytes accessed | tf_op | source)
XLA Modules:
  0.0 209.6 jit_solution(12929214142790427288)
XLA Ops:
  2.7 1.4 copy.135
  4.1 1.5 copy.94
  5.5 10.1 %all-to-all-start = ((bf16[64,2,8,1024]{3,2,1,0:T(8,128)(2,1)}), bf16[64,2,8,1024]{3,2,1,0:T(8,128)(2,1)S(1)}, u32[]{:S(2)}, u32[]{:S(2)}) async-start(bf16[64,2,8,1024]{3,2,1,0:T(8,128)(2,1)} %copy.94), calls=%async_computation | async-start | bytes 4194304 | tf_op jit(solution)/shard_map/all_to_all | solution.py:96
  15.7 48.8 %all-to-all-done = bf16[64,2,8,1024]{3,2,1,0:T(8,128)(2,1)S(1)} async-done(((bf16[64,2,8,1024]{3,2,1,0:T(8,128)(2,1)}), bf16[64,2,8,1024]{3,2,1,0:T(8,128)(2,1)S(1)}, u32[]{:S(2)}, u32[]{:S(2)}) %all-to-all-start) | async-done | bytes 2097184 | tf_op jit(solution)/shard_map/all_to_all | solution.py:96
  65.8 2.3 %copy.136 = bf16[128,8,8,128]{3,2,1,0:T(8,128)(2,1)S(1)} copy(bf16[128,8,8,128]{3,1,2,0:T(8,128)(2,1)} %bitcast.220) | data formatting | bytes 4194304
  68.1 17.3 %while.14 = (s32[]{:T(128)}, bf16[4,256,1,8,128]{4,1,3,2,0:T(8,128)(2,1)}, f32[4,256,1,8]{1,0,3,2:T(4,128)S(1)}, f32[4,256,1,8]{1,0,3,2:T(4,128)S(1)}, bf16[4,25...) while((s32[]{:T(128)}, ...), condition=%wide.region_7.8_spmd, body=%wide.region_4.7_spmd.sunk | while | flops 545779712 | bytes 15049321 | solution.py:53
  70.2 2.1 fusion.63
  74.5 2.0 fusion.63
  78.8 2.1 fusion.63
  83.2 2.0 fusion.63
  87.8 7.9 %all-to-all-start.1 = ((f32[64,1,128]{2,1,0:T(1,128)}), f32[64,1,128]{2,1,0:T(1,128)S(1)}, u32[]{:S(2)}, u32[]{:S(2)}) async-start(f32[64,1,128]{2,1,0:T(1,128)} %reshape.286), calls=%async_computation.1 | async-start | bytes 65536 | tf_op jit(solution)/shard_map/all_to_all | solution.py:38
  96.7 1.4 reshape.284
  98.1 4.6 %all-to-all-done.1 = f32[64,1,128]{2,1,0:T(1,128)S(1)} async-done(((f32[64,1,128]{2,1,0:T(1,128)}), f32[64,1,128]{2,1,0:T(1,128)S(1)}, u32[]{:S(2)}, u32[]{:S(2)}) %all-to-all-start.1) | async-done | bytes 32800 | tf_op jit(solution)/shard_map/all_to_all | solution.py:38
  102.7 7.2 %all-to-all-start.2 = ((f32[64,1,128]{2,1,0:T(1,128)}), f32[64,1,128]{2,1,0:T(1,128)S(1)}, u32[]{:S(2)}, u32[]{:S(2)}) async-start(f32[64,1,128]{2,1,0:T(1,128)} %reshape.284), calls=%async_computation.2 | async-start | bytes 65536 | tf_op jit(solution)/shard_map/all_to_all | solution.py:39
  109.9 2.9 %copy.115 = bf16[4,256,1,8,128]{4,3,1,0,2:T(8,128)(2,1)S(1)} copy(bf16[4,256,1,8,128]{4,1,3,2,0:T(8,128)(2,1)} %get-tuple-element.46) | data formatting | bytes 4194304 | tf_op jit(solution)/shard_map/convert_element_type | solution.py:36
  112.8 2.3 %reshape.235 = bf16[64,2,8,1024]{3,2,1,0:T(8,128)(2,1)} reshape(bf16[4,256,1,8,128]{4,3,1,0,2:T(8,128)(2,1)S(1)} %copy.115) | data formatting | bytes 4194304 | tf_op jit(solution)/shard_map/convert_element_type | solution.py:36
  115.2 1.7 all-to-all-done.2
  116.8 8.8 %all-to-all-start.3 = ((bf16[64,2,8,1024]{3,2,1,0:T(8,128)(2,1)}), bf16[64,2,8,1024]{3,2,1,0:T(8,128)(2,1)S(1)}, u32[]{:S(2)}, u32[]{:S(2)}) async-start(bf16[64,2,8,1024]{3,2,1,0:T(8,128)(2,1)} %reshape.235), calls=%async_computation.3 | async-start | bytes 4194304 | tf_op jit(solution)/shard_map/all_to_all | solution.py:35
  125.8 1.7 gather_fusion.3
  128.2 1.8 fusion.53
  130.2 1.9 fusion.25
  134.6 1.5 gather_fusion
  136.1 1.8 copy.122
  140.8 1.7 gather_fusion.1
  142.5 1.6 copy.124
  144.1 1.4 fusion.52
  145.8 1.7 copy.114
  147.7 26.7 %all-to-all-done.3 = bf16[64,2,8,1024]{3,2,1,0:T(8,128)(2,1)S(1)} async-done(((bf16[64,2,8,1024]{3,2,1,0:T(8,128)(2,1)}), bf16[64,2,8,1024]{3,2,1,0:T(8,128)(2,1)S(1)}, u32[]{:S(2)}, u32[]{:S(2)}) %all-to-all-start.3) | async-done | bytes 2097184 | tf_op jit(solution)/shard_map/all_to_all | solution.py:35
  174.4 1.9 copy.155
  176.3 3.7 %gather_fusion.2 = bf16[112,8,8,128]{3,2,1,0:T(8,128)(2,1)} fusion(bf16[128,8,8,128]{3,2,1,0:T(8,128)(2,1)} %copy.155, s32[1024]{0:T(1024)S(1)} %pad_clamp_fusion), kind=kCustom, calls=%fused_computation.2 | custom fusion | bytes 3670464 | tf_op jit(solution)/shard_map/gather | solution.py:105
  180.1 2.5 %fusion.23 = f32[16,8,8,128]{3,2,1,0:T(8,128)S(1)} fusion(bf16[16,7,8,8,128]{4,3,2,1,0:T(8,128)(2,1)} %bitcast.223, f32[16,7,8,8]{3,2,1,0:T(8,128)S(1)} %copy-done.3), kind=kLoop, calls=%fused_computation.25 | loop fusion | flops 2621440 | bytes 2387968 | tf_op jit(solution)/shard_map/reduce_sum | solution.py:112
  185.3 23.2 %psum.7 = f32[128]{0:T(128)S(1)} all-reduce(f32[128]{0:T(128)S(1)} %get-tuple-element.99), channel_id=1, replica_groups=mesh['ctx'=64,'head'=8] {'head'}, use_global_device_ids=true, to_apply=%region_12.13 | all-reduce | flops 128 | bytes 1024 | tf_op jit(solution)/shard_map/psum | solution.py:117
  (102 shorter events, 26.9 us)
Async XLA Ops:
  5.5 58.9 %all-to-all-start = ((bf16[64,2,8,1024]{3,2,1,0:T(8,128)(2,1)}), bf16[64,2,8,1024]{3,2,1,0:T(8,128)(2,1)S(1)}, u32[]{:S(2)}, u32[]{:S(2)}) async-start(bf16[64,2,8,1024]{3,2,1,0:T(8,128)(2,1)} %copy.94), calls=%async_computation | async-start | bytes 4194304 | tf_op jit(solution)/shard_map/all_to_all | solution.py:96
  64.5 1.3 copy-start.1
  65.8 2.3 %copy-start.2 = (bf16[512,128]{1,0:T(8,128)(2,1)S(1)}, bf16[512,128]{1,0:T(8,128)(2,1)}, u32[]{:S(2)}) copy-start(bf16[512,128]{1,0:T(8,128)(2,1)} %param.9) | copy-start | bytes 393220
  65.8 2.3 %copy-start.8 = (bf16[512,128]{1,0:T(8,128)(2,1)S(1)}, bf16[512,128]{1,0:T(8,128)(2,1)}, u32[]{:S(2)}) copy-start(bf16[512,128]{1,0:T(8,128)(2,1)} %param.10) | copy-start | bytes 393220
  87.8 14.9 %all-to-all-start.1 = ((f32[64,1,128]{2,1,0:T(1,128)}), f32[64,1,128]{2,1,0:T(1,128)S(1)}, u32[]{:S(2)}, u32[]{:S(2)}) async-start(f32[64,1,128]{2,1,0:T(1,128)} %reshape.286), calls=%async_computation.1 | async-start | bytes 65536 | tf_op jit(solution)/shard_map/all_to_all | solution.py:38
  102.7 14.1 %all-to-all-start.2 = ((f32[64,1,128]{2,1,0:T(1,128)}), f32[64,1,128]{2,1,0:T(1,128)S(1)}, u32[]{:S(2)}, u32[]{:S(2)}) async-start(f32[64,1,128]{2,1,0:T(1,128)} %reshape.284), calls=%async_computation.2 | async-start | bytes 65536 | tf_op jit(solution)/shard_map/all_to_all | solution.py:39
  115.2 10.4 %copy-start.5 = (s32[16,8]{0,1:T(8,128)S(1)}, s32[16,8]{0,1:T(8,128)}, u32[]{:S(2)}) copy-start(s32[16,8]{0,1:T(8,128)} %param.12) | copy-start | bytes 1540
  116.8 57.6 %all-to-all-start.3 = ((bf16[64,2,8,1024]{3,2,1,0:T(8,128)(2,1)}), bf16[64,2,8,1024]{3,2,1,0:T(8,128)(2,1)S(1)}, u32[]{:S(2)}, u32[]{:S(2)}) async-start(bf16[64,2,8,1024]{3,2,1,0:T(8,128)(2,1)} %reshape.235), calls=%async_computation.3 | async-start | bytes 4194304 | tf_op jit(solution)/shard_map/all_to_all | solution.py:35
  125.8 2.2 %copy-start.7 = (s32[16]{0:T(128)S(1)}, s32[16]{0:T(128)}, u32[]{:S(2)}) copy-start(s32[16]{0:T(128)} %param.11) | copy-start | bytes 196
  125.8 2.4 %copy-start.4 = (bf16[128,1024]{1,0:T(8,128)(2,1)S(1)}, bf16[128,1024]{1,0:T(8,128)(2,1)}, u32[]{:S(2)}) copy-start(bf16[128,1024]{1,0:T(8,128)(2,1)} %param.8) | copy-start | bytes 786436
  128.2 4.0 %copy-start.6 = (bf16[1024]{0:T(1024)(128)(2,1)S(1)}, bf16[1024]{0:T(1024)(128)(2,1)}, u32[]{:S(2)}) copy-start(bf16[1024]{0:T(1024)(128)(2,1)} %param.13) | copy-start | bytes 6148
  176.3 3.7 %copy-start.3 = (f32[16,7,8,8]{3,2,1,0:T(8,128)S(1)}, f32[16,7,8,8]{3,2,1,0:T(8,128)}, u32[]{:S(2)}) copy-start(f32[16,7,8,8]{3,2,1,0:T(8,128)} %copy.114) | copy-start | bytes 86020
  180.0 2.7 %copy-start = (f32[128,1,8,512]{0,3,2,1:T(8,128)S(1)}, f32[128,1,8,512]{0,3,2,1:T(8,128)}, u32[]{:S(2)}) copy-start(f32[128,1,8,512]{0,3,2,1:T(8,128)} %get-tuple-element.98) | copy-start | bytes 6291460
where the time goes:
time: 213 us; the launch traced here: 210 us
  waiting for transfers between devices  81.7 us (38%)
  local copies, waits for them, and re-layouts  41 us (19%)
  starting transfers between devices  34 us (16%)
  blocking collectives  23.2 us (11%)
  matrix products  15.2 us (7%)
  other arithmetic  14 us (7%)
    all_to_all x1, waiting for transfers between devices, body(): lax.all_to_all(outgoing, 'ctx', split_axis=0, concat_axis=0, tiled=True)  48.8 us
    all_to_all x1, waiting for transfers between devices, send_back(): lax.all_to_all(mixed_out.astype(jnp.float32), 'ctx', split_axis=0, concat...  26.7 us
    psum x1, blocking collectives, body(): squares = lax.psum(jnp.sum(attended * attended, axis=-1), 'head')  23.2 us
    unnamed x25, local copies, waits for them, and re-layouts  11.3 us
    all_to_all x1, starting transfers between devices, body(): lax.all_to_all(outgoing, 'ctx', split_axis=0, concat_axis=0, tiled=True)  10.1 us
    dot_general x5, matrix products, attend(): jnp.einsum('nkgj,jkd->nkgd', probability, value_block, preferred_element_...  9.5 us
    all_to_all x1, starting transfers between devices, send_back(): lax.all_to_all(mixed_out.astype(jnp.float32), 'ctx', split_axis=0, concat...  8.76 us
    all_to_all x1, starting transfers between devices, send_back(): lax.all_to_all(row_peak, 'ctx', split_axis=0, concat_axis=0, tiled=True)  7.9 us
  transfers between devices with their start and end apart: 4, of which 4 were waited for; matrix products, arithmetic and copies ran while one was open for 14% of the time, Pallas kernels for 0%

commit v1 on v0

v1 whole, which is shorter than its diff:
```python
import math

import jax
import jax.numpy as jnp
from jax import lax
from jax.experimental import pallas as pl
from jax.experimental.pallas import tpu as pltpu
from jax.sharding import Mesh
from jax.sharding import PartitionSpec as P

HD = 128
HEADS = 8
BLK = 512
CAP = 2
FEAT = 8192
ROWS_Y = 8
COLS_X = 4
QBLK = 16
QB = 8
QR = QB * HEADS
MSG = QBLK + 1
DUMMY = QBLK
LOW = -1e30
SCALE = math.log2(math.e) / math.sqrt(HD)

f32 = jnp.float32
bf16 = jnp.bfloat16
VMEM = pl.BlockSpec(memory_space=pltpu.VMEM)
SMEM = pl.BlockSpec(memory_space=pltpu.SMEM)


def call(kernel, outs, operands, specs, scratch=(), mib=16, flops=0, size=0):
    return pl.pallas_call(
        kernel,
        out_shape=outs,
        in_specs=specs,
        out_specs=jax.tree.map(lambda _: VMEM, outs),
        scratch_shapes=list(scratch),
        compiler_params=pltpu.CompilerParams(vmem_limit_bytes=mib * 2**20),
        cost_estimate=pl.CostEstimate(flops=flops, bytes_accessed=size, transcendentals=0),
    )(*operands)


def join_kernel(k_ref, v_ref, kv_ref):
    kv_ref[:BLK, :] = k_ref[...]
    kv_ref[BLK:, :] = v_ref[...]


def pack_kernel(q_ref, sel_ref, out_ref):
    for pair in range(QBLK // 2):
        rows = q_ref[pair * 16 : pair * 16 + 16, :].astype(f32)
        for half in range(2):
            part = rows[half * QB : half * QB + QB]
            tile = jnp.concatenate([part[:, h * HD : (h + 1) * HD] for h in range(HEADS)], axis=0).astype(bf16)
            for s in range(COLS_X):
                out_ref[s, pair * 2 + half] = tile
    sel = jnp.concatenate([sel_ref[...].astype(f32), jnp.zeros((QBLK, HD - 8), f32)], axis=1)
    tile = jnp.concatenate([sel, jnp.zeros((QR - QBLK, HD), f32)], axis=0).astype(bf16)
    for s in range(COLS_X):
        out_ref[s, QBLK] = tile


def scores_of(q, k):
    return lax.dot_general(q, k, (((1,), (1,)), ((), ())), preferred_element_type=f32) * SCALE


def with_ones(v):
    return jnp.concatenate([v, jnp.ones((BLK, HD), bf16)], axis=1)


def own_kernel(off_ref, q_ref, kv_ref, out_ref, lse_ref):
    k = kv_ref[:BLK, :]
    v = with_ones(kv_ref[BLK:, :])
    ahead = lax.broadcasted_iota(jnp.int32, (QR, BLK), 1) - lax.rem(
        lax.broadcasted_iota(jnp.int32, (QR, BLK), 0), QB
    )
    lane = lax.rem(lax.broadcasted_iota(jnp.int32, (QR, HD), 1), QBLK)
    lse = jnp.full((QR, HD), LOW, f32)
    for first in range(0, QBLK, 4):
        q = jnp.concatenate([q_ref[0, first + i] for i in range(4)], axis=0)
        s = scores_of(q, k)
        s = jnp.concatenate(
            [jnp.where(ahead <= off_ref[first + i], s[i * QR : (i + 1) * QR], LOW) for i in range(4)], axis=0
        )
        peak = jnp.max(s, axis=1, keepdims=True)
        p = jnp.exp2(s - peak).astype(bf16)
        o = jnp.dot(p, v, preferred_element_type=f32)
        total = o[:, HD:]
        mixed = o[:, :HD] / total
        entry = peak + jnp.log2(total)
        for i in range(4):
            out_ref[first + i] = mixed[i * QR : (i + 1) * QR]
            lse = jnp.where(lane == first + i, entry[i * QR : (i + 1) * QR], lse)
    lse_ref[...] = lse


def serve_kernel(index_ref, q_ref, *refs):
    blocks, (out_ref, acc, peak, total, qbuf) = refs[:-5], refs[-5:]
    acc[...] = jnp.zeros_like(acc)
    total[...] = jnp.zeros_like(total)
    peak[...] = jnp.full_like(peak, LOW)
    per = COLS_X * CAP
    j = 0
    for ref in blocks:
        for start in range(0, ref.shape[0], 2 * BLK):
            k = ref[start : start + BLK, :]
            v = with_ones(ref[start + BLK : start + 2 * BLK, :])
            for first in range(0, per, 4):
                ids = [index_ref[j * per + first + i] for i in range(4)]
                q = jnp.concatenate([q_ref[t] for t in ids], axis=0)
                s = scores_of(q, k)
                before = jnp.concatenate([peak[t] for t in ids], axis=0)
                now = jnp.maximum(before, jnp.max(s, axis=1, keepdims=True))
                p = jnp.exp2(s - jnp.concatenate([now] * (BLK // HD), axis=1)).astype(bf16)
                o = jnp.dot(p, v, preferred_element_type=f32)
                keep = jnp.exp2(before - now)
                for i, t in enumerate(ids):
                    part = slice(i * QR, (i + 1) * QR)
                    acc[t] = acc[t] * keep[part] + o[part, :HD]
                    total[t] = total[t] * keep[part] + o[part, HD:]
                    peak[t] = now[part]
            j += 1
    lanes = lax.broadcasted_iota(jnp.int32, (QR, HD), 1)
    lane = lax.rem(lanes, QBLK)
    for s in range(COLS_X):
        lse = jnp.full((QR, HD), LOW, f32)
        for g in range(QBLK):
            t = s * MSG + g
            tot = total[t]
            used = tot > 0.0
            safe = jnp.where(used, tot, 1.0)
            out_ref[s, g] = (acc[t] / safe).astype(bf16)
            lse = jnp.where(lane == g, jnp.where(used, peak[t] + jnp.log2(safe), LOW), lse)
        high = lse.astype(bf16).astype(f32)
        middle = (lse - high).astype(bf16).astype(f32)
        low = lse - high - middle
        out_ref[s, QBLK] = jnp.where(lanes < QBLK, high, jnp.where(lanes < 2 * QBLK, middle, low)).astype(bf16)


def combine_kernel(back_ref, own_ref, own_lse_ref, att_ref, squares_ref):
    lses = []
    for s in range(COLS_X):
        st = back_ref[s, QBLK].astype(f32)
        lses.append(st + pltpu.roll(st, HD - QBLK, 1) + pltpu.roll(st, HD - 2 * QBLK, 1))
    lses.append(own_lse_ref[...])
    most = lses[0]
    for e in lses[1:]:
        most = jnp.maximum(most, e)
    weights = [jnp.exp2(e - most) for e in lses]
    inverse = 1.0 / sum(weights)
    weights = [w * inverse for w in weights]
    lane = lax.broadcasted_iota(jnp.int32, (QB, HD), 1)
    squares = jnp.zeros((QB, HD), f32)
    for g in range(QBLK):
        a = weights[COLS_X][:, g : g + 1] * own_ref[g]
        for s in range(COLS_X):
            a = a + weights[s][:, g : g + 1] * back_ref[s, g].astype(f32)
        att_ref[g] = a
        sq = a * a
        rows = sq[:QB]
        for h in range(1, HEADS):
            rows = rows + sq[h * QB : (h + 1) * QB]
        squares = jnp.where(lane == g, jnp.sum(rows, axis=1, keepdims=True), squares)
    for z in range(squares_ref.shape[0]):
        squares_ref[z] = squares


def norm_kernel(att_ref, squares_ref, gain_ref, out_ref):
    squares = squares_ref[0]
    for z in range(1, squares_ref.shape[0]):
        squares = squares + squares_ref[z]
    scale = lax.rsqrt(squares * (1.0 / FEAT) + 1e-06)
    for pair in range(QBLK // 2):
        halves = []
        for g in (2 * pair, 2 * pair + 1):
            factor = jnp.broadcast_to(scale[:, g : g + 1], (QB, HD))
            halves.append(
                jnp.concatenate([att_ref[g, h * QB : (h + 1) * QB, :] * factor for h in range(HEADS)], axis=1)
            )
        rows = jnp.concatenate(halves, axis=0) * gain_ref[...].astype(f32)
        out_ref[pair * 16 : pair * 16 + 16, :] = rows.astype(bf16)


def index_of(selected, blocks):
    hit = jnp.any(selected[:, :, :, None] == blocks[None, None, None, :], axis=2)
    count = hit.astype(jnp.int32)
    earlier = jnp.tril(jnp.ones((QBLK, QBLK), jnp.int32), -1)
    rank = jnp.sum(earlier[None, :, :, None] * count[:, None, :, :], axis=2)
    name = jnp.arange(COLS_X, dtype=jnp.int32)[:, None] * MSG + jnp.arange(QBLK, dtype=jnp.int32)[None, :]
    slots = []
    for c in range(CAP):
        here = hit & (rank == c)
        slots.append(DUMMY + jnp.sum(jnp.where(here, name[:, :, None] - DUMMY, 0), axis=1))
    return jnp.stack(slots, axis=-1).transpose(1, 0, 2).reshape(-1)


def body(queries, key_cache, value_cache, offsets, selected, out_gain):
    y, x, core = lax.axis_index("y"), lax.axis_index("x"), lax.axis_index("core")
    sds = jax.ShapeDtypeStruct
    kv = call(join_kernel, sds((2 * BLK, HD), bf16), (key_cache, value_cache), [VMEM] * 2, size=2**19)

    def up(a, k):
        return lax.ppermute(a, "y", [(i, i + 1) for i in range(k - 1, ROWS_Y - 1)])

    def down(a, k):
        return lax.ppermute(a, "y", [((i - k + 1) % ROWS_Y, (i - k) % ROWS_Y) for i in range(3)])

    def swap(a):
        return lax.ppermute(a, "core", [(0, 1), (1, 0)])

    up1, down1 = up(kv, 1), down(kv, 1)
    packed = call(pack_kernel, sds((COLS_X, MSG, QR, HD), bf16), (queries, selected), [VMEM] * 2, size=2**21)
    asked = lax.all_to_all(packed, "x", split_axis=0, concat_axis=0, tiled=True)
    far = lax.ppermute(kv, "y", [(i, i + 4) for i in range(4)])
    up2, down2 = up(up1, 2), down(down1, 2)
    up3, down3 = up(up2, 3), down(down2, 3)
    group1 = jnp.concatenate([up1, down1], axis=0)
    group2 = jnp.concatenate([up2, down2, far], axis=0)
    group3 = jnp.concatenate([up3, down3], axis=0)
    held = [kv, swap(kv), group1, swap(group1), group2, swap(group2), group3, swap(group3)]
    column = []
    for shifts in ((0,), (1, 7), (2, 6, 4), (3, 5)):
        for c in (core, 1 - core):
            column += [lax.rem(y + ROWS_Y - k, ROWS_Y) * (2 * COLS_X) + x * 2 + c for k in shifts]
    own, own_lse = call(
        own_kernel,
        (sds((QBLK, QR, HD), f32), sds((QR, HD), f32)),
        (offsets, packed, kv),
        [SMEM, VMEM, VMEM],
        flops=2**28,
        size=2**21,
    )
    wanted = asked[:, QBLK, :QBLK, 1:8].astype(jnp.int32)
    index = index_of(wanted, jnp.stack(column).astype(jnp.int32))
    slots = COLS_X * MSG
    served = call(
        serve_kernel,
        sds((COLS_X, MSG, QR, HD), bf16),
        (index, asked.reshape(slots, QR, HD), *held),
        [SMEM] + [VMEM] * (1 + len(held)),
        scratch=[pltpu.VMEM((slots, QR, HD), f32)] * 3 + [pltpu.VMEM((BLK, HD), bf16)],
        mib=40,
        flops=2**31,
        size=2**23,
    )
    back = lax.all_to_all(served, "x", split_axis=0, concat_axis=0, tiled=True)
    att, squares = call(
        combine_kernel,
        (sds((QBLK, QR, HD), f32), sds((8, QB, HD), f32)),
        (back, own, own_lse),
        [VMEM] * 3,
        size=2**21,
    )
    squares = lax.all_to_all(squares, "head", split_axis=0, concat_axis=0, tiled=True)
    return call(
        norm_kernel,
        sds((QBLK * QB, HEADS * HD), bf16),
        (att, squares, out_gain.reshape(1, HEADS * HD)),
        [VMEM] * 3,
        size=2**20,
    )


def solution(mesh):
    grid = Mesh(mesh.devices.reshape(ROWS_Y, COLS_X, 2, mesh.shape["head"]), ("y", "x", "core", "head"))
    ctx = ("y", "x", "core")
    placed = (P(ctx, "head"), P(ctx, "head"), P(ctx, "head"), P(ctx), P(ctx, None), P("head"))
    return jax.shard_map(body, mesh=grid, in_specs=placed, out_specs=P(ctx, "head"), check_vma=False)
```

time: 213 us -> 100 us (0.47); the launches traced: 210 us -> 99.6 us
  waiting for transfers between devices: 81.7 us -> 36.5 us
  local copies, waits for them, and re-layouts: 41 us -> 5.13 us
  blocking collectives: 23.2 us -> 0 us
  Pallas kernels: 0 us -> 15.8 us
  matrix products: 15.2 us -> 0 us
  other arithmetic: 14 us -> 0.65 us
  starting transfers between devices: 34 us -> 41.3 us
    all_to_all x4 -> x3, waiting for transfers between devices: 81.7 us -> 21.8 us  [the longest x1 13.8 us: body(): back = lax.all_to_all(served, 'x', split_axis=0, concat_axis=0, tiled=True)]
    psum x1 -> x0, blocking collectives: 23.2 us -> none  [body(): squares = lax.psum(jnp.sum(attended * attended, axis=-1), 'head')]
    ppermute x0 -> x11, starting transfers between devices: none -> 19.9 us  [the longest x4 7.69 us: swap(): return lax.ppermute(a, 'core', [(0, 1), (1, 0)])]
    pallas_call x0 -> x6, Pallas kernels: none -> 15.8 us  [call(): pl.pallas_call(kernel, out_shape=outs, in_specs=specs, out_specs=jax.tree...]
    dot_general x11 -> x0, matrix products: 15.2 us -> none  [the longest x5 9.5 us: attend(): jnp.einsum('nkgj,jkd->nkgd', probability, value_block, preferred_element_...]
    ppermute x0 -> x11, waiting for transfers between devices: none -> 14.7 us  [the longest x3 12 us: down(): lax.ppermute(a, 'y', [((i - k + 1) % ROWS_Y, (i - k) % ROWS_Y) for i in r...]
    all_to_all x4 -> x3, starting transfers between devices: 34 us -> 21.4 us  [the longest x1 10.3 us: body(): lax.all_to_all(squares, 'head', split_axis=0, concat_axis=0, tiled=True)]
    gather x10 -> x0, local copies, waits for them, and re-layouts: 12.4 us -> none  [the longest x1 3.72 us: body(): back_mixed.reshape(devices * CAP, block_rows, head_count, HD)[flat_index]]
  transfers between devices with their start and end apart: 4 -> 14, of which waited for: 4 -> 7; matrix products, arithmetic and copies ran while one was open for 14% -> 3% of each run, Pallas kernels for 0% -> 3%
where the time goes in v1:
time: 100 us; the launch traced here: 99.6 us
  starting transfers between devices  41.3 us (41%)
  waiting for transfers between devices  36.5 us (36%)
  Pallas kernels  15.8 us (16%)
  local copies, waits for them, and re-layouts  5.13 us (5%)
    pallas_call x6, Pallas kernels, call(): pl.pallas_call(kernel, out_shape=outs, in_specs=specs, out_specs=jax.tree...  15.8 us
    all_to_all x1, waiting for transfers between devices, body(): back = lax.all_to_all(served, 'x', split_axis=0, concat_axis=0, tiled=True)  13.8 us
    ppermute x3, waiting for transfers between devices, down(): lax.ppermute(a, 'y', [((i - k + 1) % ROWS_Y, (i - k) % ROWS_Y) for i in r...  12 us
    all_to_all x1, starting transfers between devices, body(): lax.all_to_all(squares, 'head', split_axis=0, concat_axis=0, tiled=True)  10.3 us
    all_to_all x1, waiting for transfers between devices, body(): lax.all_to_all(squares, 'head', split_axis=0, concat_axis=0, tiled=True)  8.01 us
    ppermute x4, starting transfers between devices, swap(): return lax.ppermute(a, 'core', [(0, 1), (1, 0)])  7.69 us
    ppermute x3, starting transfers between devices, down(): lax.ppermute(a, 'y', [((i - k + 1) % ROWS_Y, (i - k) % ROWS_Y) for i in r...  7.06 us
    all_to_all x1, starting transfers between devices, body(): back = lax.all_to_all(served, 'x', split_axis=0, concat_axis=0, tiled=True)  6.79 us
  transfers between devices with their start and end apart: 14, of which 7 were waited for; matrix products, arithmetic and copies ran while one was open for 3% of the time, Pallas kernels for 3%

profile of v1, /device:TPU:56, one launch (start us, length us, event | category | flops | bytes accessed | tf_op | source)
XLA Modules:
  0.0 99.6 jit_solution(12503177226691889810)
XLA Ops:
  0.0 0.9 copy-done.1
  0.9 0.9 copy-done.2
  1.8 1.3 %collective-permute-start.1 = (bf16[1024,128]{1,0:T(8,128)(2,1)S(1)}, bf16[1024,128]{1,0:T(8,128)(2,1)S(1)}, u32[]{:S(2)}, u32[]{:S(2)}) collective-permute-start(bf16[1024,128]{1,0:T(8,128)(2,1)S(1)} %shard_map.65.refs_0_.kv_ref), channel_id=1, source_target_pairs={{0,64},{64,128},{128,192},{192,256},{256,320},{320,384},{384,448},... | collective-permute-start | bytes 786440 | tf_op jit(solution)/shard_map/ppermute | solution.py:203
  3.1 1.3 %collective-permute-start.2 = (bf16[1024,128]{1,0:T(8,128)(2,1)S(1)}, bf16[1024,128]{1,0:T(8,128)(2,1)S(1)}, u32[]{:S(2)}, u32[]{:S(2)}) collective-permute-start(bf16[1024,128]{1,0:T(8,128)(2,1)S(1)} %shard_map.65.refs_0_.kv_ref), channel_id=1, source_target_pairs={{0,448},{64,0},{128,64},{1,449},{65,1},{129,65},{2,450},{66,2},{13... | collective-permute-start | bytes 786440 | tf_op jit(solution)/shard_map/ppermute | solution.py:206
  4.4 1.3 %collective-permute-start.6 = (bf16[1024,128]{1,0:T(8,128)(2,1)S(1)}, bf16[1024,128]{1,0:T(8,128)(2,1)S(1)}, u32[]{:S(2)}, u32[]{:S(2)}) collective-permute-start(bf16[1024,128]{1,0:T(8,128)(2,1)S(1)} %shard_map.65.refs_0_.kv_ref), channel_id=1, source_target_pairs={{0,256},{64,320},{128,384},{192,448},{1,257},{65,321},{129,385},{1... | collective-permute-start | bytes 786440 | tf_op jit(solution)/shard_map/ppermute | solution.py:214
  5.7 1.9 %collective-permute-start = (bf16[1024,128]{1,0:T(8,128)(2,1)S(1)}, bf16[1024,128]{1,0:T(8,128)(2,1)S(1)}, u32[]{:S(2)}, u32[]{:S(2)}) collective-permute-start(bf16[1024,128]{1,0:T(8,128)(2,1)S(1)} %shard_map.65.refs_0_.kv_ref), channel_id=1, source_target_pairs={{0,8},{8,0},{1,9},{9,1},{2,10},{10,2},{3,11},{11,3},{4,12},{12,4},... | collective-permute-start | bytes 786440 | tf_op jit(solution)/shard_map/ppermute | solution.py:209
  7.7 0.8 copy.11.sel_ref
  8.4 0.9 copy-done
  9.4 1.1 %shard_map.64.q_ref = bf16[4,17,64,128]{3,2,1,0:T(8,128)(2,1)} custom-call(bf16[128,1024]{1,0:T(8,128)(2,1)S(1)} %copy-done, s32[16,8]{1,0:T(8,128)S(1)} %copy.11.sel_ref), custom_call_target="tpu_custom_call" | custom-call | bytes 2097152 | tf_op jit(solution)/shard_map/pallas_call | solution.py:33
  10.5 4.3 %all-to-all-start = ((bf16[4,17,64,128]{3,2,1,0:T(8,128)(2,1)}), bf16[4,17,64,128]{3,2,1,0:T(8,128)(2,1)S(1)}, u32[]{:S(2)}, u32[]{:S(2)}) async-start(bf16[4,17,64,128]{3,2,1,0:T(8,128)(2,1)} %shard_map.64.q_ref), calls=%async_computation | async-start | bytes 2228224 | tf_op jit(solution)/shard_map/all_to_all | solution.py:213
  14.9 1.3 %collective-permute-start.4 = (bf16[1024,128]{1,0:T(8,128)(2,1)S(1)}, bf16[1024,128]{1,0:T(8,128)(2,1)}, u32[]{:S(2)}, u32[]{:S(2)}) collective-permute-start(bf16[1024,128]{1,0:T(8,128)(2,1)S(1)} %collective-permute-done.1), channel_id=1, source_target_pairs={{64,128},{128,192},{192,256},{256,320},{320,384},{384,448},{65,129... | collective-permute-start | bytes 786440 | tf_op jit(solution)/shard_map/ppermute | solution.py:203
  16.4 5.6 %collective-permute-done.2 = bf16[1024,128]{1,0:T(8,128)(2,1)S(1)} collective-permute-done((bf16[1024,128]{1,0:T(8,128)(2,1)S(1)}, bf16[1024,128]{1,0:T(8,128)(2,1)S(1)}, u32[]{:S(2)}, u32[]{:S(2)}) %collective-permute-start.2) | collective-permute-done | bytes 262176 | tf_op jit(solution)/shard_map/ppermute | solution.py:206
  22.0 1.9 %collective-permute-start.5 = (bf16[1024,128]{1,0:T(8,128)(2,1)S(1)}, bf16[1024,128]{1,0:T(8,128)(2,1)S(1)}, u32[]{:S(2)}, u32[]{:S(2)}) collective-permute-start(bf16[1024,128]{1,0:T(8,128)(2,1)S(1)} %collective-permute-done.2), channel_id=1, source_target_pairs={{448,384},{0,448},{64,0},{449,385},{1,449},{65,1},{450,386},{2,450... | collective-permute-start | bytes 786440 | tf_op jit(solution)/shard_map/ppermute | solution.py:206
  23.9 1.9 %collective-permute-start.3 = (bf16[2048,128]{1,0:T(8,128)(2,1)S(1)}, bf16[2048,128]{1,0:T(8,128)(2,1)}, u32[]{:S(2)}, u32[]{:S(2)}) collective-permute-start(bf16[2048,128]{1,0:T(8,128)(2,1)S(1)} %constant_dynamic-update-slice_fusion.refs_2_), channel_id=1, source_target_pairs={{0,8},{8,0},{1,9},{9,1},{2,10},{10,2},{3,11},{11,3},{4,12},{12,4},... | collective-permute-start | bytes 1572872 | tf_op jit(solution)/shard_map/ppermute | solution.py:209
  25.9 1.3 %collective-permute-start.8 = (bf16[1024,128]{1,0:T(8,128)(2,1)}, bf16[1024,128]{1,0:T(8,128)(2,1)S(1)}, u32[]{:S(2)}, u32[]{:S(2)}) collective-permute-start(bf16[1024,128]{1,0:T(8,128)(2,1)} %collective-permute-done.4), channel_id=1, source_target_pairs={{128,192},{192,256},{256,320},{320,384},{384,448},{129,193},{193,2... | collective-permute-start | bytes 786440 | tf_op jit(solution)/shard_map/ppermute | solution.py:203
  27.2 1.0 constant_dynamic-update-slice_fusion.4
  28.2 4.3 %collective-permute-done.5 = bf16[1024,128]{1,0:T(8,128)(2,1)S(1)} collective-permute-done((bf16[1024,128]{1,0:T(8,128)(2,1)S(1)}, bf16[1024,128]{1,0:T(8,128)(2,1)S(1)}, u32[]{:S(2)}, u32[]{:S(2)}) %collective-permute-start.5) | collective-permute-done | bytes 262176 | tf_op jit(solution)/shard_map/ppermute | solution.py:206
  32.5 3.9 %collective-permute-start.9 = (bf16[1024,128]{1,0:T(8,128)(2,1)S(1)}, bf16[1024,128]{1,0:T(8,128)(2,1)S(1)}, u32[]{:S(2)}, u32[]{:S(2)}) collective-permute-start(bf16[1024,128]{1,0:T(8,128)(2,1)S(1)} %collective-permute-done.5), channel_id=1, source_target_pairs={{384,320},{448,384},{0,448},{385,321},{449,385},{1,449},{386,322},... | collective-permute-start | bytes 786440 | tf_op jit(solution)/shard_map/ppermute | solution.py:206
  36.4 1.9 %collective-permute-start.7 = (bf16[3072,128]{1,0:T(8,128)(2,1)S(1)}, bf16[3072,128]{1,0:T(8,128)(2,1)}, u32[]{:S(2)}, u32[]{:S(2)}) collective-permute-start(bf16[3072,128]{1,0:T(8,128)(2,1)S(1)} %constant_dynamic-update-slice_fusion.2.refs_4_), channel_id=1, source_target_pairs={{0,8},{8,0},{1,9},{9,1},{2,10},{10,2},{3,11},{11,3},{4,12},{12,4},... | collective-permute-start | bytes 2359304 | tf_op jit(solution)/shard_map/ppermute | solution.py:209
  38.4 1.6 %collective-permute-done.8 = bf16[1024,128]{1,0:T(8,128)(2,1)S(1)} collective-permute-done((bf16[1024,128]{1,0:T(8,128)(2,1)}, bf16[1024,128]{1,0:T(8,128)(2,1)S(1)}, u32[]{:S(2)}, u32[]{:S(2)}) %collective-permute-start.8) | collective-permute-done | bytes 262176 | tf_op jit(solution)/shard_map/ppermute | solution.py:203
  40.0 2.1 %collective-permute-done.9 = bf16[1024,128]{1,0:T(8,128)(2,1)S(1)} collective-permute-done((bf16[1024,128]{1,0:T(8,128)(2,1)S(1)}, bf16[1024,128]{1,0:T(8,128)(2,1)S(1)}, u32[]{:S(2)}, u32[]{:S(2)}) %collective-permute-start.9) | collective-permute-done | bytes 262176 | tf_op jit(solution)/shard_map/ppermute | solution.py:206
  42.1 1.9 %collective-permute-start.10 = (bf16[2048,128]{1,0:T(8,128)(2,1)S(1)}, bf16[2048,128]{1,0:T(8,128)(2,1)}, u32[]{:S(2)}, u32[]{:S(2)}) collective-permute-start(bf16[2048,128]{1,0:T(8,128)(2,1)S(1)} %constant_dynamic-update-slice_fusion.5.refs_6_), channel_id=1, source_target_pairs={{0,8},{8,0},{1,9},{9,1},{2,10},{10,2},{3,11},{11,3},{4,12},{12,4},... | collective-permute-start | bytes 1572872 | tf_op jit(solution)/shard_map/ppermute | solution.py:209
  44.4 0.2 multiply_reduce_fusion
  45.0 1.1 %collective-permute-done.10.refs_7_ = bf16[2048,128]{1,0:T(8,128)(2,1)} collective-permute-done((bf16[2048,128]{1,0:T(8,128)(2,1)S(1)}, bf16[2048,128]{1,0:T(8,128)(2,1)}, u32[]{:S(2)}, u32[]{:S(2)}) %collective-permute-start.10) | collective-permute-done | bytes 524320 | tf_op jit(solution)/shard_map/ppermute | solution.py:209
  46.0 9.1 %shard_map.66 = bf16[4,17,64,128]{3,2,1,0:T(8,128)(2,1)} custom-call(s32[128]{0:T(128)S(1)} %reshape.82.index_ref, bf16[68,64,128]{2,1,0:T(8,128)(2,1)S(1)} %bitcast.28, bf16[1024,128]{1,0:T(8,128)(2,1)S(1)} %shard_map.65.refs_0_.kv_ref, bf16[1024,128]{1,0:T(8,128)(2,1)S(1)} %collective-permute-done.refs_1_, ...), custom_call_target="tpu_custom_call" | custom-call | flops 2147483648 | bytes 8388608 | tf_op jit(solution)/shard_map/pallas_call | solution.py:33
  55.1 6.8 %all-to-all-start.1 = ((bf16[4,17,64,128]{3,2,1,0:T(8,128)(2,1)}), bf16[4,17,64,128]{3,2,1,0:T(8,128)(2,1)S(1)}, u32[]{:S(2)}, u32[]{:S(2)}) async-start(bf16[4,17,64,128]{3,2,1,0:T(8,128)(2,1)} %shard_map.66), calls=%async_computation.1 | async-start | bytes 2228224 | tf_op jit(solution)/shard_map/all_to_all | solution.py:246
  61.9 2.3 %shard_map.67 = (f32[16,64,128]{2,1,0:T(8,128)S(1)}, f32[64,128]{1,0:T(8,128)S(1)}) custom-call(s32[16]{0:T(128)S(1)} %copy-done.3, bf16[4,17,64,128]{3,2,1,0:T(8,128)(2,1)} %shard_map.64.q_ref, bf16[1024,128]{1,0:T(8,128)(2,1)S(1)} %shard_map.65.refs_0_.kv_ref), custom_call_target="tpu_custom_call" | custom-call | flops 268435456 | bytes 2097152 | tf_op jit(solution)/shard_map/pallas_call | solution.py:33
  64.2 13.8 %all-to-all-done.1.back_ref = bf16[4,17,64,128]{3,2,1,0:T(8,128)(2,1)S(1)} async-done(((bf16[4,17,64,128]{3,2,1,0:T(8,128)(2,1)}), bf16[4,17,64,128]{3,2,1,0:T(8,128)(2,1)S(1)}, u32[]{:S(2)}, u32[]{:S(2)}) %all-to-all-start.1) | async-done | bytes 1114144 | tf_op jit(solution)/shard_map/all_to_all | solution.py:246
  78.0 2.5 %shard_map.68 = (f32[16,64,128]{2,1,0:T(8,128)S(1)}, f32[8,8,128]{2,1,0:T(8,128)}) custom-call(bf16[4,17,64,128]{3,2,1,0:T(8,128)(2,1)S(1)} %all-to-all-done.1.back_ref, f32[16,64,128]{2,1,0:T(8,128)S(1)} %get-tuple-element.9.own_ref, f32[64,128]{1,0:T(8,128)S(1)} %get-tuple-element.10.own_lse_ref), custom_call_target="tpu_custom_call" | custom-call | bytes 2097152 | tf_op jit(solution)/shard_map/pallas_call | solution.py:33
  80.5 10.3 %all-to-all-start.2 = ((f32[8,8,128]{2,1,0:T(8,128)}), f32[8,8,128]{2,1,0:T(8,128)S(1)}, u32[]{:S(2)}, u32[]{:S(2)}) async-start(f32[8,8,128]{2,1,0:T(8,128)} %get-tuple-element.12), calls=%async_computation.2 | async-start | bytes 65536 | tf_op jit(solution)/shard_map/all_to_all | solution.py:254
  90.8 8.0 %all-to-all-done.2.squares_ref = f32[8,8,128]{2,1,0:T(8,128)S(1)} async-done(((f32[8,8,128]{2,1,0:T(8,128)}), f32[8,8,128]{2,1,0:T(8,128)S(1)}, u32[]{:S(2)}, u32[]{:S(2)}) %all-to-all-start.2) | async-done | bytes 32800 | tf_op jit(solution)/shard_map/all_to_all | solution.py:254
  98.8 0.8 shard_map.69
  (36 shorter events, 1.2 us)
Async XLA Ops:
  0.0 0.9 copy-start.1
  0.9 0.9 copy-start.2
  1.8 13.1 %collective-permute-start.1 = (bf16[1024,128]{1,0:T(8,128)(2,1)S(1)}, bf16[1024,128]{1,0:T(8,128)(2,1)S(1)}, u32[]{:S(2)}, u32[]{:S(2)}) collective-permute-start(bf16[1024,128]{1,0:T(8,128)(2,1)S(1)} %shard_map.65.refs_0_.kv_ref), channel_id=1, source_target_pairs={{0,64},{64,128},{128,192},{192,256},{256,320},{320,384},{384,448},... | collective-permute-start | bytes 786440 | tf_op jit(solution)/shard_map/ppermute | solution.py:203
  3.1 18.8 %collective-permute-start.2 = (bf16[1024,128]{1,0:T(8,128)(2,1)S(1)}, bf16[1024,128]{1,0:T(8,128)(2,1)S(1)}, u32[]{:S(2)}, u32[]{:S(2)}) collective-permute-start(bf16[1024,128]{1,0:T(8,128)(2,1)S(1)} %shard_map.65.refs_0_.kv_ref), channel_id=1, source_target_pairs={{0,448},{64,0},{128,64},{1,449},{65,1},{129,65},{2,450},{66,2},{13... | collective-permute-start | bytes 786440 | tf_op jit(solution)/shard_map/ppermute | solution.py:206
  4.4 32.0 %collective-permute-start.6 = (bf16[1024,128]{1,0:T(8,128)(2,1)S(1)}, bf16[1024,128]{1,0:T(8,128)(2,1)S(1)}, u32[]{:S(2)}, u32[]{:S(2)}) collective-permute-start(bf16[1024,128]{1,0:T(8,128)(2,1)S(1)} %shard_map.65.refs_0_.kv_ref), channel_id=1, source_target_pairs={{0,256},{64,320},{128,384},{192,448},{1,257},{65,321},{129,385},{1... | collective-permute-start | bytes 786440 | tf_op jit(solution)/shard_map/ppermute | solution.py:214
  5.7 39.2 %collective-permute-start = (bf16[1024,128]{1,0:T(8,128)(2,1)S(1)}, bf16[1024,128]{1,0:T(8,128)(2,1)S(1)}, u32[]{:S(2)}, u32[]{:S(2)}) collective-permute-start(bf16[1024,128]{1,0:T(8,128)(2,1)S(1)} %shard_map.65.refs_0_.kv_ref), channel_id=1, source_target_pairs={{0,8},{8,0},{1,9},{9,1},{2,10},{10,2},{3,11},{11,3},{4,12},{12,4},... | collective-permute-start | bytes 786440 | tf_op jit(solution)/shard_map/ppermute | solution.py:209
  8.4 0.9 copy-start
  10.5 33.5 %all-to-all-start = ((bf16[4,17,64,128]{3,2,1,0:T(8,128)(2,1)}), bf16[4,17,64,128]{3,2,1,0:T(8,128)(2,1)S(1)}, u32[]{:S(2)}, u32[]{:S(2)}) async-start(bf16[4,17,64,128]{3,2,1,0:T(8,128)(2,1)} %shard_map.64.q_ref), calls=%async_computation | async-start | bytes 2228224 | tf_op jit(solution)/shard_map/all_to_all | solution.py:213
  14.9 11.0 %collective-permute-start.4 = (bf16[1024,128]{1,0:T(8,128)(2,1)S(1)}, bf16[1024,128]{1,0:T(8,128)(2,1)}, u32[]{:S(2)}, u32[]{:S(2)}) collective-permute-start(bf16[1024,128]{1,0:T(8,128)(2,1)S(1)} %collective-permute-done.1), channel_id=1, source_target_pairs={{64,128},{128,192},{192,256},{256,320},{320,384},{384,448},{65,129... | collective-permute-start | bytes 786440 | tf_op jit(solution)/shard_map/ppermute | solution.py:203
  22.0 10.5 %collective-permute-start.5 = (bf16[1024,128]{1,0:T(8,128)(2,1)S(1)}, bf16[1024,128]{1,0:T(8,128)(2,1)S(1)}, u32[]{:S(2)}, u32[]{:S(2)}) collective-permute-start(bf16[1024,128]{1,0:T(8,128)(2,1)S(1)} %collective-permute-done.2), channel_id=1, source_target_pairs={{448,384},{0,448},{64,0},{449,385},{1,449},{65,1},{450,386},{2,450... | collective-permute-start | bytes 786440 | tf_op jit(solution)/shard_map/ppermute | solution.py:206
  23.9 21.0 %collective-permute-start.3 = (bf16[2048,128]{1,0:T(8,128)(2,1)S(1)}, bf16[2048,128]{1,0:T(8,128)(2,1)}, u32[]{:S(2)}, u32[]{:S(2)}) collective-permute-start(bf16[2048,128]{1,0:T(8,128)(2,1)S(1)} %constant_dynamic-update-slice_fusion.refs_2_), channel_id=1, source_target_pairs={{0,8},{8,0},{1,9},{9,1},{2,10},{10,2},{3,11},{11,3},{4,12},{12,4},... | collective-permute-start | bytes 1572872 | tf_op jit(solution)/shard_map/ppermute | solution.py:209
  25.9 14.1 %collective-permute-start.8 = (bf16[1024,128]{1,0:T(8,128)(2,1)}, bf16[1024,128]{1,0:T(8,128)(2,1)S(1)}, u32[]{:S(2)}, u32[]{:S(2)}) collective-permute-start(bf16[1024,128]{1,0:T(8,128)(2,1)} %collective-permute-done.4), channel_id=1, source_target_pairs={{128,192},{192,256},{256,320},{320,384},{384,448},{129,193},{193,2... | collective-permute-start | bytes 786440 | tf_op jit(solution)/shard_map/ppermute | solution.py:203
  32.5 9.6 %collective-permute-start.9 = (bf16[1024,128]{1,0:T(8,128)(2,1)S(1)}, bf16[1024,128]{1,0:T(8,128)(2,1)S(1)}, u32[]{:S(2)}, u32[]{:S(2)}) collective-permute-start(bf16[1024,128]{1,0:T(8,128)(2,1)S(1)} %collective-permute-done.5), channel_id=1, source_target_pairs={{384,320},{448,384},{0,448},{385,321},{449,385},{1,449},{386,322},... | collective-permute-start | bytes 786440 | tf_op jit(solution)/shard_map/ppermute | solution.py:206
  36.4 8.5 %collective-permute-start.7 = (bf16[3072,128]{1,0:T(8,128)(2,1)S(1)}, bf16[3072,128]{1,0:T(8,128)(2,1)}, u32[]{:S(2)}, u32[]{:S(2)}) collective-permute-start(bf16[3072,128]{1,0:T(8,128)(2,1)S(1)} %constant_dynamic-update-slice_fusion.2.refs_4_), channel_id=1, source_target_pairs={{0,8},{8,0},{1,9},{9,1},{2,10},{10,2},{3,11},{11,3},{4,12},{12,4},... | collective-permute-start | bytes 2359304 | tf_op jit(solution)/shard_map/ppermute | solution.py:209
  42.1 3.9 %collective-permute-start.10 = (bf16[2048,128]{1,0:T(8,128)(2,1)S(1)}, bf16[2048,128]{1,0:T(8,128)(2,1)}, u32[]{:S(2)}, u32[]{:S(2)}) collective-permute-start(bf16[2048,128]{1,0:T(8,128)(2,1)S(1)} %constant_dynamic-update-slice_fusion.5.refs_6_), channel_id=1, source_target_pairs={{0,8},{8,0},{1,9},{9,1},{2,10},{10,2},{3,11},{11,3},{4,12},{12,4},... | collective-permute-start | bytes 1572872 | tf_op jit(solution)/shard_map/ppermute | solution.py:209
  55.1 6.8 %copy-start.3 = (s32[16]{0:T(128)S(1)}, s32[16]{0:T(128)}, u32[]{:S(2)}) copy-start(s32[16]{0:T(128)} %off_ref.1) | copy-start | bytes 196
  55.1 22.9 %all-to-all-start.1 = ((bf16[4,17,64,128]{3,2,1,0:T(8,128)(2,1)}), bf16[4,17,64,128]{3,2,1,0:T(8,128)(2,1)S(1)}, u32[]{:S(2)}, u32[]{:S(2)}) async-start(bf16[4,17,64,128]{3,2,1,0:T(8,128)(2,1)} %shard_map.66), calls=%async_computation.1 | async-start | bytes 2228224 | tf_op jit(solution)/shard_map/all_to_all | solution.py:246
  64.2 26.6 %copy-start.4 = (bf16[1024]{0:T(1024)(128)(2,1)S(1)}, bf16[1024]{0:T(1024)(128)(2,1)}, u32[]{:S(2)}) copy-start(bf16[1024]{0:T(1024)(128)(2,1)} %param.11) | copy-start | bytes 6148
  80.5 18.3 %all-to-all-start.2 = ((f32[8,8,128]{2,1,0:T(8,128)}), f32[8,8,128]{2,1,0:T(8,128)S(1)}, u32[]{:S(2)}, u32[]{:S(2)}) async-start(f32[8,8,128]{2,1,0:T(8,128)} %get-tuple-element.12), calls=%async_computation.2 | async-start | bytes 65536 | tf_op jit(solution)/shard_map/all_to_all | solution.py:254

commit v2 on v1

--- a/solution.py
+++ b/solution.py
@@ -29,21 +29,42 @@
 SMEM = pl.BlockSpec(memory_space=pltpu.SMEM)
 
 
-def call(kernel, outs, operands, specs, scratch=(), mib=16, flops=0, size=0):
+def call(kernel, outs, operands, specs, mib=16, flops=0, size=0, aliases=None, scratch=()):
     return pl.pallas_call(
         kernel,
         out_shape=outs,
         in_specs=specs,
         out_specs=jax.tree.map(lambda _: VMEM, outs),
         scratch_shapes=list(scratch),
+        input_output_aliases=aliases or {},
         compiler_params=pltpu.CompilerParams(vmem_limit_bytes=mib * 2**20),
         cost_estimate=pl.CostEstimate(flops=flops, bytes_accessed=size, transcendentals=0),
     )(*operands)
 
 
-def join_kernel(k_ref, v_ref, kv_ref):
-    kv_ref[:BLK, :] = k_ref[...]
-    kv_ref[BLK:, :] = v_ref[...]
+def join_kernel(*refs):
+    *parts, out_ref, sems = refs
+    copies = []
+    row = 0
+    for i, ref in enumerate(parts):
+        copies.append(pltpu.make_async_copy(ref, out_ref.at[row : row + ref.shape[0], :], sems.at[i]))
+        row += ref.shape[0]
+    for copy in copies:
+        copy.start()
+    for copy in copies:
+        copy.wait()
+
+
+def join(parts):
+    return call(
+        join_kernel,
+        jax.ShapeDtypeStruct((sum(p.shape[0] for p in parts), HD), bf16),
+        parts,
+        [pl.BlockSpec(memory_space=pl.ANY)] * len(parts),
+        mib=63,
+        size=2**20,
+        scratch=[pltpu.SemaphoreType.DMA((len(parts),))],
+    )
 
 
 def pack_kernel(q_ref, sel_ref, out_ref):
@@ -68,14 +89,15 @@
     return jnp.concatenate([v, jnp.ones((BLK, HD), bf16)], axis=1)
 
 
-def own_kernel(off_ref, q_ref, kv_ref, out_ref, lse_ref):
+def own_kernel(off_ref, q_ref, kv_ref, out_ref, peak_ref, total_ref):
     k = kv_ref[:BLK, :]
     v = with_ones(kv_ref[BLK:, :])
     ahead = lax.broadcasted_iota(jnp.int32, (QR, BLK), 1) - lax.rem(
         lax.broadcasted_iota(jnp.int32, (QR, BLK), 0), QB
     )
-    lane = lax.rem(lax.broadcasted_iota(jnp.int32, (QR, HD), 1), QBLK)
-    lse = jnp.full((QR, HD), LOW, f32)
+    lane = lax.broadcasted_iota(jnp.int32, (QR, HD), 1)
+    peaks = jnp.zeros((QR, HD), f32)
+    totals = jnp.ones((QR, HD), f32)
     for first in range(0, QBLK, 4):
         q = jnp.concatenate([q_ref[0, first + i] for i in range(4)], axis=0)
         s = scores_of(q, k)
@@ -85,22 +107,18 @@
         peak = jnp.max(s, axis=1, keepdims=True)
         p = jnp.exp2(s - peak).astype(bf16)
         o = jnp.dot(p, v, preferred_element_type=f32)
-        total = o[:, HD:]
-        mixed = o[:, :HD] / total
-        entry = peak + jnp.log2(total)
         for i in range(4):
-            out_ref[first + i] = mixed[i * QR : (i + 1) * QR]
-            lse = jnp.where(lane == first + i, entry[i * QR : (i + 1) * QR], lse)
-    lse_ref[...] = lse
-
-
-def serve_kernel(index_ref, q_ref, *refs):
-    blocks, (out_ref, acc, peak, total, qbuf) = refs[:-5], refs[-5:]
-    acc[...] = jnp.zeros_like(acc)
-    total[...] = jnp.zeros_like(total)
-    peak[...] = jnp.full_like(peak, LOW)
+            part = slice(i * QR, (i + 1) * QR)
+            out_ref[first + i] = o[part, :HD]
+            peaks = jnp.where(lane == first + i, peak[part], peaks)
+            totals = jnp.where(lane == first + i, o[part, HD:], totals)
+    peak_ref[...] = peaks
+    total_ref[...] = totals
+
+
+def merge(index_ref, first_block, q_ref, blocks, acc, peak, total):
     per = COLS_X * CAP
-    j = 0
+    j = first_block
     for ref in blocks:
         for start in range(0, ref.shape[0], 2 * BLK):
             k = ref[start : start + BLK, :]
@@ -120,41 +138,49 @@
                     total[t] = total[t] * keep[part] + o[part, HD:]
                     peak[t] = now[part]
             j += 1
+
+
+def serve_kernel(index_ref, q_ref, *refs):
+    *blocks, out_ref, acc, peak, total = refs
+    acc[...] = jnp.zeros_like(acc)
+    total[...] = jnp.zeros_like(total)
+    peak[...] = jnp.full_like(peak, LOW)
+    merge(index_ref, 0, q_ref, blocks, acc, peak, total)
     lanes = lax.broadcasted_iota(jnp.int32, (QR, HD), 1)
     lane = lax.rem(lanes, QBLK)
+    term = lax.rem(lax.div(lanes, QBLK), 3)
     for s in range(COLS_X):
-        lse = jnp.full((QR, HD), LOW, f32)
+        both = jnp.zeros((QR, HD), f32)
         for g in range(QBLK):
             t = s * MSG + g
-            tot = total[t]
-            used = tot > 0.0
-            safe = jnp.where(used, tot, 1.0)
-            out_ref[s, g] = (acc[t] / safe).astype(bf16)
-            lse = jnp.where(lane == g, jnp.where(used, peak[t] + jnp.log2(safe), LOW), lse)
-        high = lse.astype(bf16).astype(f32)
-        middle = (lse - high).astype(bf16).astype(f32)
-        low = lse - high - middle
-        out_ref[s, QBLK] = jnp.where(lanes < QBLK, high, jnp.where(lanes < 2 * QBLK, middle, low)).astype(bf16)
-
-
-def combine_kernel(back_ref, own_ref, own_lse_ref, att_ref, squares_ref):
-    lses = []
+            out_ref[s, g] = acc[t].astype(bf16)
+            both = jnp.where(lane == g, jnp.where(lanes < 3 * QBLK, peak[t], total[t]), both)
+        high = both.astype(bf16).astype(f32)
+        middle = (both - high).astype(bf16).astype(f32)
+        low = both - high - middle
+        out_ref[s, QBLK] = jnp.where(term == 0, high, jnp.where(term == 1, middle, low)).astype(bf16)
+
+
+def combine_kernel(back_ref, own_ref, own_peak_ref, own_total_ref, att_ref, squares_ref):
+    peaks = [own_peak_ref[...]]
+    totals = [own_total_ref[...]]
     for s in range(COLS_X):
-        st = back_ref[s, QBLK].astype(f32)
-        lses.append(st + pltpu.roll(st, HD - QBLK, 1) + pltpu.roll(st, HD - 2 * QBLK, 1))
-    lses.append(own_lse_ref[...])
-    most = lses[0]
-    for e in lses[1:]:
+        terms = back_ref[s, QBLK].astype(f32)
+        both = terms + pltpu.roll(terms, HD - QBLK, 1) + pltpu.roll(terms, HD - 2 * QBLK, 1)
+        peaks.append(both)
+        totals.append(pltpu.roll(both, HD - 3 * QBLK, 1))
+    most = peaks[0]
+    for e in peaks[1:]:
         most = jnp.maximum(most, e)
-    weights = [jnp.exp2(e - most) for e in lses]
-    inverse = 1.0 / sum(weights)
+    weights = [jnp.exp2(e - most) for e in peaks]
+    inverse = 1.0 / sum(w * t for w, t in zip(weights, totals))
     weights = [w * inverse for w in weights]
     lane = lax.broadcasted_iota(jnp.int32, (QB, HD), 1)
     squares = jnp.zeros((QB, HD), f32)
     for g in range(QBLK):
-        a = weights[COLS_X][:, g : g + 1] * own_ref[g]
+        a = weights[0][:, g : g + 1] * own_ref[g]
         for s in range(COLS_X):
-            a = a + weights[s][:, g : g + 1] * back_ref[s, g].astype(f32)
+            a = a + weights[s + 1][:, g : g + 1] * back_ref[s, g].astype(f32)
         att_ref[g] = a
         sq = a * a
         rows = sq[:QB]
@@ -197,7 +223,7 @@
 def body(queries, key_cache, value_cache, offsets, selected, out_gain):
     y, x, core = lax.axis_index("y"), lax.axis_index("x"), lax.axis_index("core")
     sds = jax.ShapeDtypeStruct
-    kv = call(join_kernel, sds((2 * BLK, HD), bf16), (key_cache, value_cache), [VMEM] * 2, size=2**19)
+    kv = join((key_cache, value_cache))
 
     def up(a, k):
         return lax.ppermute(a, "y", [(i, i + 1) for i in range(k - 1, ROWS_Y - 1)])
@@ -211,20 +237,24 @@
     up1, down1 = up(kv, 1), down(kv, 1)
     packed = call(pack_kernel, sds((COLS_X, MSG, QR, HD), bf16), (queries, selected), [VMEM] * 2, size=2**21)
     asked = lax.all_to_all(packed, "x", split_axis=0, concat_axis=0, tiled=True)
-    far = lax.ppermute(kv, "y", [(i, i + 4) for i in range(4)])
-    up2, down2 = up(up1, 2), down(down1, 2)
-    up3, down3 = up(up2, 3), down(down2, 3)
-    group1 = jnp.concatenate([up1, down1], axis=0)
-    group2 = jnp.concatenate([up2, down2, far], axis=0)
-    group3 = jnp.concatenate([up3, down3], axis=0)
-    held = [kv, swap(kv), group1, swap(group1), group2, swap(group2), group3, swap(group3)]
+    far = lax.ppermute(kv, "y", [(2, 6), (3, 7)])
+    down2 = lax.ppermute(kv, "y", [(0, 6), (1, 7), (2, 0)])
+    up2 = up(up1, 2)
+    round_back = lax.ppermute(down2, "y", [(6, 4), (7, 5)])
+    down3 = down(down2, 3)
+    far, up2 = lax.optimization_barrier((far, up2))
+    up3 = up(up2, 3)
+    held = [kv, swap(kv)]
+    for group in ((up1, down1, down2), (up2, down3), (up3, jnp.where(y < 6, round_back, far))):
+        group = jnp.concatenate(group, axis=0) if len(group) > 1 else group[0]
+        held += [group, swap(group)]
     column = []
-    for shifts in ((0,), (1, 7), (2, 6, 4), (3, 5)):
+    for shifts in ((0,), (1, 7, 6), (2, 5), (3, 4)):
         for c in (core, 1 - core):
             column += [lax.rem(y + ROWS_Y - k, ROWS_Y) * (2 * COLS_X) + x * 2 + c for k in shifts]
-    own, own_lse = call(
+    own = call(
         own_kernel,
-        (sds((QBLK, QR, HD), f32), sds((QR, HD), f32)),
+        (sds((QBLK, QR, HD), f32), sds((QR, HD), f32), sds((QR, HD), f32)),
         (offsets, packed, kv),
         [SMEM, VMEM, VMEM],
         flops=2**28,
@@ -233,22 +263,23 @@
     wanted = asked[:, QBLK, :QBLK, 1:8].astype(jnp.int32)
     index = index_of(wanted, jnp.stack(column).astype(jnp.int32))
     slots = COLS_X * MSG
+    asked = asked.reshape(slots, QR, HD)
     served = call(
         serve_kernel,
         sds((COLS_X, MSG, QR, HD), bf16),
-        (index, asked.reshape(slots, QR, HD), *held),
+        (index, asked, *held),
         [SMEM] + [VMEM] * (1 + len(held)),
-        scratch=[pltpu.VMEM((slots, QR, HD), f32)] * 3 + [pltpu.VMEM((BLK, HD), bf16)],
-        mib=40,
-        flops=2**31,
+        mib=32,
+        flops=16 * 2**27,
         size=2**23,
+        scratch=[pltpu.VMEM((slots, QR, HD), f32)] * 3,
     )
     back = lax.all_to_all(served, "x", split_axis=0, concat_axis=0, tiled=True)
     att, squares = call(
         combine_kernel,
         (sds((QBLK, QR, HD), f32), sds((8, QB, HD), f32)),
-        (back, own, own_lse),
-        [VMEM] * 3,
+        (back, *own),
+        [VMEM] * 4,
         size=2**21,
     )
     squares = lax.all_to_all(squares, "head", split_axis=0, concat_axis=0, tiled=True)

time: 100 us -> 104 us (1.040)
  waiting for transfers between devices: 36.5 us -> 44.5 us
  starting transfers between devices: 41.3 us -> 37.8 us
  local copies, waits for them, and re-layouts: 5.13 us -> 2.33 us
  Pallas kernels: 15.8 us -> 17.1 us
    ppermute x1 -> x3, waiting for transfers between devices: 0.01 us -> 10.9 us  [the longest x1 10.9 us: body(): down2 = lax.ppermute(kv, 'y', [(0, 6), (1, 7), (2, 0)])]
    ppermute x3 -> x2, starting transfers between devices: 7.06 us -> 3.2 us  [down(): lax.ppermute(a, 'y', [((i - k + 1) % ROWS_Y, (i - k) % ROWS_Y) for i in r...]
    unnamed x15 -> x16, local copies, waits for them, and re-layouts: 4.57 us -> 1.81 us
    ppermute x1 -> x3, starting transfers between devices: 1.29 us -> 3.88 us  [the longest x1 1.29 us: body(): round_back = lax.ppermute(down2, 'y', [(6, 4), (7, 5)])]
    all_to_all x1, starting transfers between devices: 6.79 us -> 4.42 us  [body(): back = lax.all_to_all(served, 'x', split_axis=0, concat_axis=0, tiled=True)]
    ppermute x3 -> x2, waiting for transfers between devices: 12 us -> 9.62 us  [down(): lax.ppermute(a, 'y', [((i - k + 1) % ROWS_Y, (i - k) % ROWS_Y) for i in r...]
    pallas_call x6, Pallas kernels: 15.8 us -> 17.1 us  [call(): pl.pallas_call(kernel, out_shape=outs, in_specs=specs, out_specs=jax.tree...]
  transfers between devices with their start and end apart: 14 -> 15, of which waited for: 7 -> 7; matrix products, arithmetic and copies ran while one was open for 3% -> 2% of each run, Pallas kernels for 3% -> 3%
where the time goes in v2:
time: 104 us; the launch traced here: 103 us
  waiting for transfers between devices  44.5 us (43%)
  starting transfers between devices  37.8 us (36%)
  Pallas kernels  17.1 us (16%)
  local copies, waits for them, and re-layouts  2.33 us (2%)
    pallas_call x6, Pallas kernels, call(): pl.pallas_call(kernel, out_shape=outs, in_specs=specs, out_specs=jax.tree...  17.1 us
    all_to_all x1, waiting for transfers between devices, body(): back = lax.all_to_all(served, 'x', split_axis=0, concat_axis=0, tiled=True)  13.8 us
    ppermute x1, waiting for transfers between devices, body(): down2 = lax.ppermute(kv, 'y', [(0, 6), (1, 7), (2, 0)])  10.9 us
    all_to_all x1, starting transfers between devices, body(): lax.all_to_all(squares, 'head', split_axis=0, concat_axis=0, tiled=True)  10.3 us
    ppermute x2, waiting for transfers between devices, down(): lax.ppermute(a, 'y', [((i - k + 1) % ROWS_Y, (i - k) % ROWS_Y) for i in r...  9.62 us
    all_to_all x1, waiting for transfers between devices, body(): lax.all_to_all(squares, 'head', split_axis=0, concat_axis=0, tiled=True)  8.01 us
    ppermute x4, starting transfers between devices, swap(): return lax.ppermute(a, 'core', [(0, 1), (1, 0)])  7.82 us
    all_to_all x1, starting transfers between devices, body(): back = lax.all_to_all(served, 'x', split_axis=0, concat_axis=0, tiled=True)  4.42 us
  transfers between devices with their start and end apart: 15, of which 7 were waited for; matrix products, arithmetic and copies ran while one was open for 2% of the time, Pallas kernels for 3%

profile of v2, /device:TPU:56, one launch (start us, length us, event | category | flops | bytes accessed | tf_op | source)
XLA Modules:
  0.0 102.8 jit_solution(4762530320552422826)
XLA Ops:
  0.0 1.7 %shard_map.65.refs_0_.kv_ref = bf16[1024,128]{1,0:T(8,128)(2,1)} custom-call(bf16[512,128]{1,0:T(8,128)(2,1)} %refs_0_.1, bf16[512,128]{1,0:T(8,128)(2,1)} %refs_1_.1), custom_call_target="tpu_custom_call" | custom-call | bytes 1048576 | tf_op jit(solution)/shard_map/pallas_call | solution.py:33
  1.7 1.3 %collective-permute-start.1 = (bf16[1024,128]{1,0:T(8,128)(2,1)}, bf16[1024,128]{1,0:T(8,128)(2,1)S(1)}, u32[]{:S(2)}, u32[]{:S(2)}) collective-permute-start(bf16[1024,128]{1,0:T(8,128)(2,1)} %shard_map.65.refs_0_.kv_ref), channel_id=1, source_target_pairs={{0,64},{64,128},{128,192},{192,256},{256,320},{320,384},{384,448},... | collective-permute-start | bytes 786440 | tf_op jit(solution)/shard_map/ppermute | solution.py:229
  3.0 1.3 %collective-permute-start.5 = (bf16[1024,128]{1,0:T(8,128)(2,1)}, bf16[1024,128]{1,0:T(8,128)(2,1)S(1)}, u32[]{:S(2)}, u32[]{:S(2)}) collective-permute-start(bf16[1024,128]{1,0:T(8,128)(2,1)} %shard_map.65.refs_0_.kv_ref), channel_id=1, source_target_pairs={{128,384},{192,448},{129,385},{193,449},{130,386},{194,450},{131,3... | collective-permute-start | bytes 786440 | tf_op jit(solution)/shard_map/ppermute | solution.py:240
  4.3 1.3 %collective-permute-start.3 = (bf16[1024,128]{1,0:T(8,128)(2,1)}, bf16[1024,128]{1,0:T(8,128)(2,1)S(1)}, u32[]{:S(2)}, u32[]{:S(2)}) collective-permute-start(bf16[1024,128]{1,0:T(8,128)(2,1)} %shard_map.65.refs_0_.kv_ref), channel_id=1, source_target_pairs={{0,384},{64,448},{128,0},{1,385},{65,449},{129,1},{2,386},{66,450}... | collective-permute-start | bytes 786440 | tf_op jit(solution)/shard_map/ppermute | solution.py:241
  5.6 1.3 %collective-permute-start.2 = (bf16[1024,128]{1,0:T(8,128)(2,1)}, bf16[1024,128]{1,0:T(8,128)(2,1)S(1)}, u32[]{:S(2)}, u32[]{:S(2)}) collective-permute-start(bf16[1024,128]{1,0:T(8,128)(2,1)} %shard_map.65.refs_0_.kv_ref), channel_id=1, source_target_pairs={{0,448},{64,0},{128,64},{1,449},{65,1},{129,65},{2,450},{66,2},{13... | collective-permute-start | bytes 786440 | tf_op jit(solution)/shard_map/ppermute | solution.py:232
  6.9 1.9 %collective-permute-start = (bf16[1024,128]{1,0:T(8,128)(2,1)}, bf16[1024,128]{1,0:T(8,128)(2,1)S(1)}, u32[]{:S(2)}, u32[]{:S(2)}) collective-permute-start(bf16[1024,128]{1,0:T(8,128)(2,1)} %shard_map.65.refs_0_.kv_ref), channel_id=1, source_target_pairs={{0,8},{8,0},{1,9},{9,1},{2,10},{10,2},{3,11},{11,3},{4,12},{12,4},... | collective-permute-start | bytes 786440 | tf_op jit(solution)/shard_map/ppermute | solution.py:235
  8.8 0.8 copy.11.sel_ref
  9.6 0.9 copy-done.1
  10.5 1.2 %shard_map.64.q_ref = bf16[4,17,64,128]{3,2,1,0:T(8,128)(2,1)} custom-call(bf16[128,1024]{1,0:T(8,128)(2,1)S(1)} %copy-done.1, s32[16,8]{1,0:T(8,128)S(1)} %copy.11.sel_ref), custom_call_target="tpu_custom_call" | custom-call | bytes 2097152 | tf_op jit(solution)/shard_map/pallas_call | solution.py:33
  11.7 4.3 %all-to-all-start = ((bf16[4,17,64,128]{3,2,1,0:T(8,128)(2,1)}), bf16[4,17,64,128]{3,2,1,0:T(8,128)(2,1)S(1)}, u32[]{:S(2)}, u32[]{:S(2)}) async-start(bf16[4,17,64,128]{3,2,1,0:T(8,128)(2,1)} %shard_map.64.q_ref), calls=%async_computation | async-start | bytes 2228224 | tf_op jit(solution)/shard_map/all_to_all | solution.py:239
  16.2 1.3 %collective-permute-start.6 = (bf16[1024,128]{1,0:T(8,128)(2,1)S(1)}, bf16[1024,128]{1,0:T(8,128)(2,1)S(1)}, u32[]{:S(2)}, u32[]{:S(2)}) collective-permute-start(bf16[1024,128]{1,0:T(8,128)(2,1)S(1)} %collective-permute-done.1), channel_id=1, source_target_pairs={{64,128},{128,192},{192,256},{256,320},{320,384},{384,448},{65,129... | collective-permute-start | bytes 786440 | tf_op jit(solution)/shard_map/ppermute | solution.py:229
  17.6 10.9 %collective-permute-done.3 = bf16[1024,128]{1,0:T(8,128)(2,1)S(1)} collective-permute-done((bf16[1024,128]{1,0:T(8,128)(2,1)}, bf16[1024,128]{1,0:T(8,128)(2,1)S(1)}, u32[]{:S(2)}, u32[]{:S(2)}) %collective-permute-start.3) | collective-permute-done | bytes 262176 | tf_op jit(solution)/shard_map/ppermute | solution.py:241
  28.5 1.3 %collective-permute-start.10 = (bf16[1024,128]{1,0:T(8,128)(2,1)S(1)}, bf16[1024,128]{1,0:T(8,128)(2,1)S(1)}, u32[]{:S(2)}, u32[]{:S(2)}) collective-permute-start(bf16[1024,128]{1,0:T(8,128)(2,1)S(1)} %collective-permute-done.3), channel_id=1, source_target_pairs={{384,256},{448,320},{385,257},{449,321},{386,258},{450,322},{387,2... | collective-permute-start | bytes 786440 | tf_op jit(solution)/shard_map/ppermute | solution.py:243
  29.8 3.6 %collective-permute-done.2 = bf16[1024,128]{1,0:T(8,128)(2,1)S(1)} collective-permute-done((bf16[1024,128]{1,0:T(8,128)(2,1)}, bf16[1024,128]{1,0:T(8,128)(2,1)S(1)}, u32[]{:S(2)}, u32[]{:S(2)}) %collective-permute-start.2) | collective-permute-done | bytes 262176 | tf_op jit(solution)/shard_map/ppermute | solution.py:232
  33.4 1.9 %collective-permute-start.7 = (bf16[1024,128]{1,0:T(8,128)(2,1)S(1)}, bf16[1024,128]{1,0:T(8,128)(2,1)S(1)}, u32[]{:S(2)}, u32[]{:S(2)}) collective-permute-start(bf16[1024,128]{1,0:T(8,128)(2,1)S(1)} %collective-permute-done.3), channel_id=1, source_target_pairs={{384,320},{448,384},{0,448},{385,321},{449,385},{1,449},{386,322},... | collective-permute-start | bytes 786440 | tf_op jit(solution)/shard_map/ppermute | solution.py:232
  35.4 1.9 %collective-permute-start.4 = (bf16[3072,128]{1,0:T(8,128)(2,1)S(1)}, bf16[3072,128]{1,0:T(8,128)(2,1)}, u32[]{:S(2)}, u32[]{:S(2)}) collective-permute-start(bf16[3072,128]{1,0:T(8,128)(2,1)S(1)} %constant_dynamic-update-slice_fusion.refs_2_), channel_id=1, source_target_pairs={{0,8},{8,0},{1,9},{9,1},{2,10},{10,2},{3,11},{11,3},{4,12},{12,4},... | collective-permute-start | bytes 2359304 | tf_op jit(solution)/shard_map/ppermute | solution.py:235
  37.4 1.3 %collective-permute-start.9 = (bf16[1024,128]{1,0:T(8,128)(2,1)S(1)}, bf16[1024,128]{1,0:T(8,128)(2,1)S(1)}, u32[]{:S(2)}, u32[]{:S(2)}) collective-permute-start(bf16[1024,128]{1,0:T(8,128)(2,1)S(1)} %collective-permute-done.6), channel_id=1, source_target_pairs={{128,192},{192,256},{256,320},{320,384},{384,448},{129,193},{193,2... | collective-permute-start | bytes 786440 | tf_op jit(solution)/shard_map/ppermute | solution.py:229
  38.7 6.0 %collective-permute-done.7 = bf16[1024,128]{1,0:T(8,128)(2,1)S(1)} collective-permute-done((bf16[1024,128]{1,0:T(8,128)(2,1)S(1)}, bf16[1024,128]{1,0:T(8,128)(2,1)S(1)}, u32[]{:S(2)}, u32[]{:S(2)}) %collective-permute-start.7) | collective-permute-done | bytes 262176 | tf_op jit(solution)/shard_map/ppermute | solution.py:232
  44.8 2.1 %collective-permute-start.8 = (bf16[2048,128]{1,0:T(8,128)(2,1)S(1)}, bf16[2048,128]{1,0:T(8,128)(2,1)}, u32[]{:S(2)}, u32[]{:S(2)}) collective-permute-start(bf16[2048,128]{1,0:T(8,128)(2,1)S(1)} %constant_dynamic-update-slice_fusion.3.refs_4_), channel_id=1, source_target_pairs={{0,8},{8,0},{1,9},{9,1},{2,10},{10,2},{3,11},{11,3},{4,12},{12,4},... | collective-permute-start | bytes 1572872 | tf_op jit(solution)/shard_map/ppermute | solution.py:235
  46.9 1.1 %collective-permute-done.9 = bf16[1024,128]{1,0:T(8,128)(2,1)S(1)} collective-permute-done((bf16[1024,128]{1,0:T(8,128)(2,1)S(1)}, bf16[1024,128]{1,0:T(8,128)(2,1)S(1)}, u32[]{:S(2)}, u32[]{:S(2)}) %collective-permute-start.9) | collective-permute-done | bytes 262176 | tf_op jit(solution)/shard_map/ppermute | solution.py:229
  48.0 1.9 %collective-permute-start.11 = (bf16[2048,128]{1,0:T(8,128)(2,1)S(1)}, bf16[2048,128]{1,0:T(8,128)(2,1)}, u32[]{:S(2)}, u32[]{:S(2)}) collective-permute-start(bf16[2048,128]{1,0:T(8,128)(2,1)S(1)} %pad_maximum_fusion.refs_6_), channel_id=1, source_target_pairs={{0,8},{8,0},{1,9},{9,1},{2,10},{10,2},{3,11},{11,3},{4,12},{12,4},... | collective-permute-start | bytes 1572872 | tf_op jit(solution)/shard_map/ppermute | solution.py:235
  50.3 0.2 multiply_reduce_fusion
  50.7 0.1 reshape.82.index_ref
  50.9 1.1 %collective-permute-done.11.refs_7_ = bf16[2048,128]{1,0:T(8,128)(2,1)} collective-permute-done((bf16[2048,128]{1,0:T(8,128)(2,1)S(1)}, bf16[2048,128]{1,0:T(8,128)(2,1)}, u32[]{:S(2)}, u32[]{:S(2)}) %collective-permute-start.11) | collective-permute-done | bytes 524320 | tf_op jit(solution)/shard_map/ppermute | solution.py:235
  52.0 8.7 %shard_map.66 = bf16[4,17,64,128]{3,2,1,0:T(8,128)(2,1)} custom-call(s32[128]{0:T(128)S(1)} %reshape.82.index_ref, bf16[68,64,128]{2,1,0:T(8,128)(2,1)S(1)} %bitcast.28, bf16[1024,128]{1,0:T(8,128)(2,1)S(1)} %copy-done, bf16[1024,128]{1,0:T(8,128)(2,1)S(1)} %collective-permute-done.refs_1_, bf16[3072,128]{1,0:T(8,128)(2,1)S(1)} %constant_dynamic-update-slice_fusion.refs_2_, ...), custom_call_target="tpu_custom_call" | custom-call | flops 2147483648 | bytes 8388608 | tf_op jit(solution)/shard_map/pallas_call | solution.py:33
  60.7 4.4 %all-to-all-start.1 = ((bf16[4,17,64,128]{3,2,1,0:T(8,128)(2,1)}), bf16[4,17,64,128]{3,2,1,0:T(8,128)(2,1)S(1)}, u32[]{:S(2)}, u32[]{:S(2)}) async-start(bf16[4,17,64,128]{3,2,1,0:T(8,128)(2,1)} %shard_map.66), calls=%async_computation.1 | async-start | bytes 2228224 | tf_op jit(solution)/shard_map/all_to_all | solution.py:277
  65.1 2.3 %shard_map.67 = (f32[16,64,128]{2,1,0:T(8,128)S(1)}, f32[64,128]{1,0:T(8,128)S(1)}, f32[64,128]{1,0:T(8,128)S(1)}) custom-call(s32[16]{0:T(128)S(1)} %copy-done.2, bf16[4,17,64,128]{3,2,1,0:T(8,128)(2,1)} %shard_map.64.q_ref, bf16[1024,128]{1,0:T(8,128)(2,1)S(1)} %copy-done), custom_call_target="tpu_custom_call" | custom-call | flops 268435456 | bytes 2097152 | tf_op jit(solution)/shard_map/pallas_call | solution.py:33
  67.4 13.8 %all-to-all-done.1.back_ref = bf16[4,17,64,128]{3,2,1,0:T(8,128)(2,1)S(1)} async-done(((bf16[4,17,64,128]{3,2,1,0:T(8,128)(2,1)}), bf16[4,17,64,128]{3,2,1,0:T(8,128)(2,1)S(1)}, u32[]{:S(2)}, u32[]{:S(2)}) %all-to-all-start.1) | async-done | bytes 1114144 | tf_op jit(solution)/shard_map/all_to_all | solution.py:277
  81.2 2.5 %shard_map.68 = (f32[16,64,128]{2,1,0:T(8,128)S(1)}, f32[8,8,128]{2,1,0:T(8,128)}) custom-call(bf16[4,17,64,128]{3,2,1,0:T(8,128)(2,1)S(1)} %all-to-all-done.1.back_ref, f32[16,64,128]{2,1,0:T(8,128)S(1)} %get-tuple-element.14.own_ref, f32[64,128]{1,0:T(8,128)S(1)} %get-tuple-element.15.own_peak_ref, f32[64,128]{1,0:T(8,128)S(1)} %get-tuple-element.16.own_total_ref), custom_call_target="tpu_custom_call" | custom-call | bytes 2097152 | tf_op jit(solution)/shard_map/pallas_call | solution.py:33
  83.7 10.3 %all-to-all-start.2 = ((f32[8,8,128]{2,1,0:T(8,128)}), f32[8,8,128]{2,1,0:T(8,128)S(1)}, u32[]{:S(2)}, u32[]{:S(2)}) async-start(f32[8,8,128]{2,1,0:T(8,128)} %get-tuple-element.18), calls=%async_computation.2 | async-start | bytes 65536 | tf_op jit(solution)/shard_map/all_to_all | solution.py:285
  94.0 8.0 %all-to-all-done.2.squares_ref = f32[8,8,128]{2,1,0:T(8,128)S(1)} async-done(((f32[8,8,128]{2,1,0:T(8,128)}), f32[8,8,128]{2,1,0:T(8,128)S(1)}, u32[]{:S(2)}, u32[]{:S(2)}) %all-to-all-start.2) | async-done | bytes 32800 | tf_op jit(solution)/shard_map/all_to_all | solution.py:285
  102.0 0.8 shard_map.69
  (40 shorter events, 1.0 us)
Async XLA Ops:
  1.7 14.5 %collective-permute-start.1 = (bf16[1024,128]{1,0:T(8,128)(2,1)}, bf16[1024,128]{1,0:T(8,128)(2,1)S(1)}, u32[]{:S(2)}, u32[]{:S(2)}) collective-permute-start(bf16[1024,128]{1,0:T(8,128)(2,1)} %shard_map.65.refs_0_.kv_ref), channel_id=1, source_target_pairs={{0,64},{64,128},{128,192},{192,256},{256,320},{320,384},{384,448},... | collective-permute-start | bytes 786440 | tf_op jit(solution)/shard_map/ppermute | solution.py:229
  3.0 32.4 %collective-permute-start.5 = (bf16[1024,128]{1,0:T(8,128)(2,1)}, bf16[1024,128]{1,0:T(8,128)(2,1)S(1)}, u32[]{:S(2)}, u32[]{:S(2)}) collective-permute-start(bf16[1024,128]{1,0:T(8,128)(2,1)} %shard_map.65.refs_0_.kv_ref), channel_id=1, source_target_pairs={{128,384},{192,448},{129,385},{193,449},{130,386},{194,450},{131,3... | collective-permute-start | bytes 786440 | tf_op jit(solution)/shard_map/ppermute | solution.py:240
  4.3 24.2 %collective-permute-start.3 = (bf16[1024,128]{1,0:T(8,128)(2,1)}, bf16[1024,128]{1,0:T(8,128)(2,1)S(1)}, u32[]{:S(2)}, u32[]{:S(2)}) collective-permute-start(bf16[1024,128]{1,0:T(8,128)(2,1)} %shard_map.65.refs_0_.kv_ref), channel_id=1, source_target_pairs={{0,384},{64,448},{128,0},{1,385},{65,449},{129,1},{2,386},{66,450}... | collective-permute-start | bytes 786440 | tf_op jit(solution)/shard_map/ppermute | solution.py:241
  5.6 27.8 %collective-permute-start.2 = (bf16[1024,128]{1,0:T(8,128)(2,1)}, bf16[1024,128]{1,0:T(8,128)(2,1)S(1)}, u32[]{:S(2)}, u32[]{:S(2)}) collective-permute-start(bf16[1024,128]{1,0:T(8,128)(2,1)} %shard_map.65.refs_0_.kv_ref), channel_id=1, source_target_pairs={{0,448},{64,0},{128,64},{1,449},{65,1},{129,65},{2,450},{66,2},{13... | collective-permute-start | bytes 786440 | tf_op jit(solution)/shard_map/ppermute | solution.py:232
  6.9 44.0 %collective-permute-start = (bf16[1024,128]{1,0:T(8,128)(2,1)}, bf16[1024,128]{1,0:T(8,128)(2,1)S(1)}, u32[]{:S(2)}, u32[]{:S(2)}) collective-permute-start(bf16[1024,128]{1,0:T(8,128)(2,1)} %shard_map.65.refs_0_.kv_ref), channel_id=1, source_target_pairs={{0,8},{8,0},{1,9},{9,1},{2,10},{10,2},{3,11},{11,3},{4,12},{12,4},... | collective-permute-start | bytes 786440 | tf_op jit(solution)/shard_map/ppermute | solution.py:235
  9.6 0.9 copy-start.1
  11.7 38.3 %all-to-all-start = ((bf16[4,17,64,128]{3,2,1,0:T(8,128)(2,1)}), bf16[4,17,64,128]{3,2,1,0:T(8,128)(2,1)S(1)}, u32[]{:S(2)}, u32[]{:S(2)}) async-start(bf16[4,17,64,128]{3,2,1,0:T(8,128)(2,1)} %shard_map.64.q_ref), calls=%async_computation | async-start | bytes 2228224 | tf_op jit(solution)/shard_map/all_to_all | solution.py:239
  16.2 21.1 %collective-permute-start.6 = (bf16[1024,128]{1,0:T(8,128)(2,1)S(1)}, bf16[1024,128]{1,0:T(8,128)(2,1)S(1)}, u32[]{:S(2)}, u32[]{:S(2)}) collective-permute-start(bf16[1024,128]{1,0:T(8,128)(2,1)S(1)} %collective-permute-done.1), channel_id=1, source_target_pairs={{64,128},{128,192},{192,256},{256,320},{320,384},{384,448},{65,129... | collective-permute-start | bytes 786440 | tf_op jit(solution)/shard_map/ppermute | solution.py:229
  28.5 18.4 %collective-permute-start.10 = (bf16[1024,128]{1,0:T(8,128)(2,1)S(1)}, bf16[1024,128]{1,0:T(8,128)(2,1)S(1)}, u32[]{:S(2)}, u32[]{:S(2)}) collective-permute-start(bf16[1024,128]{1,0:T(8,128)(2,1)S(1)} %collective-permute-done.3), channel_id=1, source_target_pairs={{384,256},{448,320},{385,257},{449,321},{386,258},{450,322},{387,2... | collective-permute-start | bytes 786440 | tf_op jit(solution)/shard_map/ppermute | solution.py:243
  33.4 11.3 %collective-permute-start.7 = (bf16[1024,128]{1,0:T(8,128)(2,1)S(1)}, bf16[1024,128]{1,0:T(8,128)(2,1)S(1)}, u32[]{:S(2)}, u32[]{:S(2)}) collective-permute-start(bf16[1024,128]{1,0:T(8,128)(2,1)S(1)} %collective-permute-done.3), channel_id=1, source_target_pairs={{384,320},{448,384},{0,448},{385,321},{449,385},{1,449},{386,322},... | collective-permute-start | bytes 786440 | tf_op jit(solution)/shard_map/ppermute | solution.py:232
  35.4 2.0 %copy-start.3 = (bf16[1024,128]{1,0:T(8,128)(2,1)}, bf16[1024,128]{1,0:T(8,128)(2,1)S(1)}, u32[]{:S(2)}) copy-start(bf16[1024,128]{1,0:T(8,128)(2,1)S(1)} %collective-permute-done.5) | copy-start | bytes 786436
  35.4 15.4 %collective-permute-start.4 = (bf16[3072,128]{1,0:T(8,128)(2,1)S(1)}, bf16[3072,128]{1,0:T(8,128)(2,1)}, u32[]{:S(2)}, u32[]{:S(2)}) collective-permute-start(bf16[3072,128]{1,0:T(8,128)(2,1)S(1)} %constant_dynamic-update-slice_fusion.refs_2_), channel_id=1, source_target_pairs={{0,8},{8,0},{1,9},{9,1},{2,10},{10,2},{3,11},{11,3},{4,12},{12,4},... | collective-permute-start | bytes 2359304 | tf_op jit(solution)/shard_map/ppermute | solution.py:235
  37.4 10.6 %collective-permute-start.9 = (bf16[1024,128]{1,0:T(8,128)(2,1)S(1)}, bf16[1024,128]{1,0:T(8,128)(2,1)S(1)}, u32[]{:S(2)}, u32[]{:S(2)}) collective-permute-start(bf16[1024,128]{1,0:T(8,128)(2,1)S(1)} %collective-permute-done.6), channel_id=1, source_target_pairs={{128,192},{192,256},{256,320},{320,384},{384,448},{129,193},{193,2... | collective-permute-start | bytes 786440 | tf_op jit(solution)/shard_map/ppermute | solution.py:229
  38.7 8.2 %copy-start.4 = (bf16[1024,128]{1,0:T(8,128)(2,1)S(1)}, bf16[1024,128]{1,0:T(8,128)(2,1)}, u32[]{:S(2)}) copy-start(bf16[1024,128]{1,0:T(8,128)(2,1)} %copy-done.3) | copy-start | bytes 786436
  44.8 7.2 %copy-start = (bf16[1024,128]{1,0:T(8,128)(2,1)S(1)}, bf16[1024,128]{1,0:T(8,128)(2,1)}, u32[]{:S(2)}) copy-start(bf16[1024,128]{1,0:T(8,128)(2,1)} %shard_map.65.refs_0_.kv_ref) | copy-start | bytes 786436
  44.8 6.1 %collective-permute-start.8 = (bf16[2048,128]{1,0:T(8,128)(2,1)S(1)}, bf16[2048,128]{1,0:T(8,128)(2,1)}, u32[]{:S(2)}, u32[]{:S(2)}) collective-permute-start(bf16[2048,128]{1,0:T(8,128)(2,1)S(1)} %constant_dynamic-update-slice_fusion.3.refs_4_), channel_id=1, source_target_pairs={{0,8},{8,0},{1,9},{9,1},{2,10},{10,2},{3,11},{11,3},{4,12},{12,4},... | collective-permute-start | bytes 1572872 | tf_op jit(solution)/shard_map/ppermute | solution.py:235
  48.0 3.9 %collective-permute-start.11 = (bf16[2048,128]{1,0:T(8,128)(2,1)S(1)}, bf16[2048,128]{1,0:T(8,128)(2,1)}, u32[]{:S(2)}, u32[]{:S(2)}) collective-permute-start(bf16[2048,128]{1,0:T(8,128)(2,1)S(1)} %pad_maximum_fusion.refs_6_), channel_id=1, source_target_pairs={{0,8},{8,0},{1,9},{9,1},{2,10},{10,2},{3,11},{11,3},{4,12},{12,4},... | collective-permute-start | bytes 1572872 | tf_op jit(solution)/shard_map/ppermute | solution.py:235
  60.7 4.4 %copy-start.2 = (s32[16]{0:T(128)S(1)}, s32[16]{0:T(128)}, u32[]{:S(2)}) copy-start(s32[16]{0:T(128)} %off_ref.1) | copy-start | bytes 196
  60.7 20.5 %all-to-all-start.1 = ((bf16[4,17,64,128]{3,2,1,0:T(8,128)(2,1)}), bf16[4,17,64,128]{3,2,1,0:T(8,128)(2,1)S(1)}, u32[]{:S(2)}, u32[]{:S(2)}) async-start(bf16[4,17,64,128]{3,2,1,0:T(8,128)(2,1)} %shard_map.66), calls=%async_computation.1 | async-start | bytes 2228224 | tf_op jit(solution)/shard_map/all_to_all | solution.py:277
  67.4 26.6 %copy-start.5 = (bf16[1024]{0:T(1024)(128)(2,1)S(1)}, bf16[1024]{0:T(1024)(128)(2,1)}, u32[]{:S(2)}) copy-start(bf16[1024]{0:T(1024)(128)(2,1)} %param.11) | copy-start | bytes 6148
  83.7 18.3 %all-to-all-start.2 = ((f32[8,8,128]{2,1,0:T(8,128)}), f32[8,8,128]{2,1,0:T(8,128)S(1)}, u32[]{:S(2)}, u32[]{:S(2)}) async-start(f32[8,8,128]{2,1,0:T(8,128)} %get-tuple-element.18), calls=%async_computation.2 | async-start | bytes 65536 | tf_op jit(solution)/shard_map/all_to_all | solution.py:285
